TPU v7x, 256 devices: a whole 4x4x8 slice. The times are simulated.
256 devices in a mesh: prefix: 32 (over y, z_lo, core), sample: 8 (over x, z_hi).
Axes of the slice: x: 4, y: 4, z: 8 (z_hi: 2, z_lo: 4; z = z_hi * 4 + z_lo), core: 2. Of those that a mesh axis runs over, the one named last changes fastest.
Arguments:
- queries: bfloat16 [256, 2, 8192], P(('prefix', 'sample')), may hold values from -100 to 100
- prefix_kv: bfloat16 [131072, 8, 256], P('prefix', 'sample'), may hold values from -8 to 8
- suffix_kv: bfloat16 [256, 1024, 8, 256], P(('prefix', 'sample')), may hold values from -10 to 10
- new_kv: bfloat16 [256, 2, 8, 256], P(('prefix', 'sample')), may hold values from -8 to 8
- lengths: int32 [256], P(('prefix', 'sample')), may hold values from 1 to 1024, 163840 in all
Outputs:
- attention: bfloat16 [256, 2, 8192], P(('prefix', 'sample'))
Inputs may be any that keep to these rules, and one draw needn't show every extreme that they name: A sample's cache holds its entries in its first lengths slots; the others are not read.
All inputs are finite; a program needn't handle non-finite values. No bound on the sum of `lengths` on one device may be relied on, other than what follows from the above.
Results may differ from a plain program's by a relative error of at most 0.0024.
Values may be sent and summed in bfloat16 or wider, within the bound.
No kernel may reach another device: no remote copies, remote signals or barrier semaphores. Data moves between devices by JAX's collectives and lax.ppermute only.
A program may use at most 128 MiB of HBM per device.

v0:
```python
import math

import jax
import jax.numpy as jnp
from jax import lax
from jax.sharding import PartitionSpec as P


def prefix_partials(query_rows, head_kv, inverse_root):
    head_dim = head_kv.shape[1] // 2
    keys_part = head_kv[:, :head_dim]
    values_part = head_kv[:, head_dim:]
    row_count = query_rows.shape[0]
    block_rows = 1024

    def one_block(rows_block):
        scores = (
            jnp.einsum("rd,pd->rp", rows_block, keys_part, preferred_element_type=jnp.float32)
            * inverse_root
        )
        block_peak = jnp.max(scores, axis=1)
        weights = jnp.exp(scores - block_peak[:, None])
        block_total = jnp.sum(weights, axis=1)
        block_numer = jnp.dot(
            weights.astype(jnp.bfloat16), values_part, preferred_element_type=jnp.float32
        )
        return (block_peak, block_total, block_numer)

    peaks, totals, numers = lax.map(
        one_block, query_rows.reshape(row_count // block_rows, block_rows, head_dim)
    )
    return (
        peaks.reshape(row_count),
        totals.reshape(row_count),
        numers.reshape(row_count, head_dim),
    )


def local_partials(query_one, suffix_one, new_one, length_one, inverse_root):
    slots = suffix_one.shape[0]
    steps_count = new_one.shape[0]
    kv_count = suffix_one.shape[1]
    head_dim = suffix_one.shape[2] // 2
    query_heads = query_one.reshape(steps_count, kv_count, -1, head_dim)
    cached = jnp.concatenate([suffix_one, new_one], axis=0)
    scores = (
        jnp.einsum(
            "tkgd,lkd->tkgl",
            query_heads,
            cached[..., :head_dim],
            preferred_element_type=jnp.float32,
        )
        * inverse_root
    )
    positions = jnp.arange(slots + steps_count)
    valid = jnp.where(
        positions[None, :] < slots,
        positions[None, :] < length_one,
        (positions - slots)[None, :] <= jnp.arange(steps_count)[:, None],
    )
    masked = jnp.where(valid[:, None, None, :], scores, -1e30)
    local_max = jnp.max(masked, axis=-1)
    weights = jnp.exp(masked - local_max[..., None])
    local_total = jnp.sum(weights, axis=-1)
    local_numer = jnp.einsum(
        "tkgl,lkd->tkgd",
        weights.astype(jnp.bfloat16),
        cached[..., head_dim:],
        preferred_element_type=jnp.float32,
    )
    return (local_max, local_total, local_numer)


def per_device(queries, prefix_kv, suffix_kv, new_kv, lengths):
    head_dim = prefix_kv.shape[2] // 2
    local_heads = prefix_kv.shape[1]
    all_heads = suffix_kv.shape[2]
    group_size = queries.shape[2] // (head_dim * all_heads)
    owned = queries.shape[0]
    steps_count = queries.shape[1]
    inverse_root = 1.0 / math.sqrt(head_dim)
    own_heads = lax.all_to_all(queries, "sample", split_axis=2, concat_axis=0, tiled=True)
    everyone = lax.all_gather(own_heads, "prefix", axis=0, tiled=True)
    samples_all = everyone.shape[0]
    by_head = everyone.reshape(
        samples_all, steps_count, local_heads, group_size, head_dim
    ).transpose(2, 0, 1, 3, 4)
    by_head = by_head.reshape(local_heads, samples_all * steps_count * group_size, head_dim)

    def head_work(paired):
        return prefix_partials(paired[0], paired[1], inverse_root)

    peaks, totals, numers = lax.map(head_work, (by_head, prefix_kv.transpose(1, 0, 2)))
    peaks = peaks.reshape(local_heads, samples_all, steps_count, group_size).transpose(1, 2, 0, 3)
    totals = totals.reshape(local_heads, samples_all, steps_count, group_size).transpose(1, 2, 0, 3)
    numers = numers.reshape(local_heads, samples_all, steps_count, group_size, head_dim).transpose(
        1, 2, 0, 3, 4
    )
    holders = lax.axis_size("prefix")
    owned_rows = samples_all // holders
    got_numer, got_peak, got_total = (
        lax.all_to_all(numers, "prefix", split_axis=0, concat_axis=0, tiled=True),
        lax.all_to_all(peaks, "prefix", split_axis=0, concat_axis=0, tiled=True),
        lax.all_to_all(totals, "prefix", split_axis=0, concat_axis=0, tiled=True),
    )
    got_numer = got_numer.reshape(
        holders, owned_rows, steps_count, local_heads, group_size, head_dim
    )
    got_peak = got_peak.reshape(holders, owned_rows, steps_count, local_heads, group_size)
    got_total = got_total.reshape(holders, owned_rows, steps_count, local_heads, group_size)
    head_peak = jnp.max(got_peak, axis=0)
    factor = jnp.exp(got_peak - head_peak)
    head_total = jnp.sum(got_total * factor, axis=0)
    head_numer = jnp.sum(got_numer * factor[..., None], axis=0)
    back_numer, back_peak, back_total = (
        lax.all_to_all(head_numer, "sample", split_axis=0, concat_axis=2, tiled=True),
        lax.all_to_all(head_peak, "sample", split_axis=0, concat_axis=2, tiled=True),
        lax.all_to_all(head_total, "sample", split_axis=0, concat_axis=2, tiled=True),
    )

    def sample_work(paired):
        return local_partials(paired[0], paired[1], paired[2], paired[3], inverse_root)

    local_max, local_total, local_numer = lax.map(
        sample_work, (queries, suffix_kv, new_kv, lengths)
    )
    overall = jnp.maximum(back_peak, local_max)
    prefix_factor = jnp.exp(back_peak - overall)
    local_factor = jnp.exp(local_max - overall)
    numerator = back_numer * prefix_factor[..., None] + local_numer * local_factor[..., None]
    denominator = back_total * prefix_factor + local_total * local_factor
    attention = numerator / denominator[..., None]
    return attention.reshape(owned, steps_count, -1).astype(jnp.bfloat16)


def solution(mesh):
    in_specs = (
        P(("prefix", "sample"), None, None),
        P("prefix", "sample", None),
        P(("prefix", "sample"), None, None, None),
        P(("prefix", "sample"), None, None, None),
        P(("prefix", "sample")),
    )
    out_specs = P(("prefix", "sample"), None, None)
    return jax.shard_map(
        per_device, mesh=mesh, in_specs=in_specs, out_specs=out_specs, check_vma=False
    )
```

profile of v0, /device:TPU:32, one launch (start us, length us, event | category | flops | bytes accessed | tf_op | source)
XLA Modules:
  0.0 372.7 jit_solution(485098632483642184)
XLA Ops:
  6.5 8.2 %copy.62 = bf16[1,2,8192]{1,0,2:T(2,128)(2,1)} copy(bf16[1,2,8192]{2,1,0:T(2,128)(2,1)} %param.7) | data formatting | bytes 65536 | tf_op args[0]
  14.8 0.5 broadcast.125
  15.3 45.2 %reduce.3 = bf16[8192,2]{1,0:T(8,128)(2,1)S(1)} reduce(bf16[8192,1,2]{2,1,0:T(2,128)(2,1)} %bitcast.140, bf16[]{:T(256)} %broadcast.125), dimensions={1}, to_apply=%bitcast.100.reduce_sub_computation | reduce | bytes 65538
  60.5 3.2 reshape.247
  63.7 20.0 %all_to_all.87 = bf16[8,2,1024]{2,1,0:T(2,128)(2,1)S(1)} all-to-all(bf16[8,2,1024]{2,1,0:T(2,128)(2,1)S(1)} %reshape.247), channel_id=1, replica_groups=mesh['prefix'=32,'sample'=8] {'sample'}, dimensions={0} | all-to-all | bytes 65536 | tf_op jit(solution)/shard_map/all_to_all | solution.py:82
  83.7 6.3 %reshape.248 = bf16[8192,1,2]{2,1,0:T(2,128)(2,1)} reshape(bf16[8,2,1024]{2,1,0:T(2,128)(2,1)S(1)} %all_to_all.87) | data formatting | bytes 65536
  90.0 8.1 %copy.63 = bf16[1,2,8192]{2,1,0:T(2,128)(2,1)S(1)} copy(bf16[1,2,8192]{1,0,2:T(2,128)(2,1)} %bitcast.141) | data formatting | bytes 65536 | tf_op jit(solution)/shard_map/all_to_all | solution.py:82
  98.1 0.6 copy.64
  98.8 1.1 fusion.50
  99.9 54.0 %all-gather.3.cloned.1.call-done = bf16[256,1,2,1024]{3,2,1,0:T(2,128)(2,1)} async-done(((bf16[8,1,2,1024]{3,2,1,0:T(2,128)(2,1)}), bf16[256,1,2,1024]{3,2,1,0:T(2,128)(2,1)}) %all-gather.3.cloned.1.call-update) | async-done | bytes 1048592 | tf_op jit(solution)/shard_map/all_gather | solution.py:83
  153.9 1.7 reshape.237
  155.7 83.1 %while.19 = (s32[]{:T(128)}, f32[4,1024]{1,0:T(4,128)S(1)}, f32[4,1024]{1,0:T(4,128)S(1)}, f32[4,1024,128]{2,1,0:T(8,128)}, bf16[4,1024,128]{2,1,0:T(8,128)(2,1)...) while((s32[]{:T(128)}, f32[4,1024]{1,0:T(4,128)S(1)}, ...), condition=%wide.region_3.4_spmd, body=%wide.region_0.3_spmd.sunk | while | flops 2181036032 | bytes 124551832 | solution.py:29
  155.7 2.4 multiply_reduce_fusion.4
  158.1 5.7 %copy-done = f32[1024,4096]{1,0:T(8,128)} copy-done((f32[1024,4096]{1,0:T(8,128)}, f32[1024,4096]{1,0:T(8,128)S(1)}, u32[]{:S(2)}) %copy-start) | copy-done | bytes 16777240 | tf_op jit(solution)/shard_map/while/body/eval_jaxpr/while
  163.8 3.8 %fusion.63 = f32[4,1024,128]{2,1,0:T(8,128)} fusion(f32[4,1024,128]{2,1,0:T(8,128)} %get-tuple-element.173, s32[]{:T(128)} %get-tuple-element.170, bf16[4096,128]{1,0:T(8,128)(2,1)S(1)} %copy-done.3, f32[1024,4096]{1,0:T(8,128)S(1)} %get-tuple-element.160, f32[1024]{0:T(1024)S(1)} %get-tuple-element.159), kind=kOutput, calls=%fused_computation.6.clone.1 | convolution fusion | flops 1086324736 | bytes 18354688 | tf_op jit(solution)/shard_map/while/body/eval_jaxpr/while/body/eval_jaxpr/dot_general | solution.py:24
  167.6 8.6 %fusion.62 = f32[1024]{0:T(1024)S(1)} fusion(f32[1024,4096]{1,0:T(8,128)} %copy-done, f32[1024]{0:T(1024)S(1)} %get-tuple-element.159), kind=kLoop, calls=%fused_computation.3.clone.1 | loop fusion | flops 12581888 | bytes 16785408 | tf_op jit(solution)/shard_map/while/body/eval_jaxpr/while/body/eval_jaxpr/reduce_sum | solution.py:23
  176.2 0.1 dynamic_update_slice.33
  176.3 0.1 dynamic_update_slice.32
  176.4 2.4 multiply_reduce_fusion.4
  178.9 5.7 %copy-done = f32[1024,4096]{1,0:T(8,128)} copy-done((f32[1024,4096]{1,0:T(8,128)}, f32[1024,4096]{1,0:T(8,128)S(1)}, u32[]{:S(2)}) %copy-start) | copy-done | bytes 16777240 | tf_op jit(solution)/shard_map/while/body/eval_jaxpr/while
  184.6 3.8 %fusion.63 = f32[4,1024,128]{2,1,0:T(8,128)} fusion(f32[4,1024,128]{2,1,0:T(8,128)} %get-tuple-element.173, s32[]{:T(128)} %get-tuple-element.170, bf16[4096,128]{1,0:T(8,128)(2,1)S(1)} %copy-done.3, f32[1024,4096]{1,0:T(8,128)S(1)} %get-tuple-element.160, f32[1024]{0:T(1024)S(1)} %get-tuple-element.159), kind=kOutput, calls=%fused_computation.6.clone.1 | convolution fusion | flops 1086324736 | bytes 18354688 | tf_op jit(solution)/shard_map/while/body/eval_jaxpr/while/body/eval_jaxpr/dot_general | solution.py:24
  188.4 8.6 %fusion.62 = f32[1024]{0:T(1024)S(1)} fusion(f32[1024,4096]{1,0:T(8,128)} %copy-done, f32[1024]{0:T(1024)S(1)} %get-tuple-element.159), kind=kLoop, calls=%fused_computation.3.clone.1 | loop fusion | flops 12581888 | bytes 16785408 | tf_op jit(solution)/shard_map/while/body/eval_jaxpr/while/body/eval_jaxpr/reduce_sum | solution.py:23
  197.0 0.1 dynamic_update_slice.33
  197.1 0.1 dynamic_update_slice.32
  197.2 2.4 multiply_reduce_fusion.4
  199.6 5.7 %copy-done = f32[1024,4096]{1,0:T(8,128)} copy-done((f32[1024,4096]{1,0:T(8,128)}, f32[1024,4096]{1,0:T(8,128)S(1)}, u32[]{:S(2)}) %copy-start) | copy-done | bytes 16777240 | tf_op jit(solution)/shard_map/while/body/eval_jaxpr/while
  205.3 3.8 %fusion.63 = f32[4,1024,128]{2,1,0:T(8,128)} fusion(f32[4,1024,128]{2,1,0:T(8,128)} %get-tuple-element.173, s32[]{:T(128)} %get-tuple-element.170, bf16[4096,128]{1,0:T(8,128)(2,1)S(1)} %copy-done.3, f32[1024,4096]{1,0:T(8,128)S(1)} %get-tuple-element.160, f32[1024]{0:T(1024)S(1)} %get-tuple-element.159), kind=kOutput, calls=%fused_computation.6.clone.1 | convolution fusion | flops 1086324736 | bytes 18354688 | tf_op jit(solution)/shard_map/while/body/eval_jaxpr/while/body/eval_jaxpr/dot_general | solution.py:24
  209.2 8.6 %fusion.62 = f32[1024]{0:T(1024)S(1)} fusion(f32[1024,4096]{1,0:T(8,128)} %copy-done, f32[1024]{0:T(1024)S(1)} %get-tuple-element.159), kind=kLoop, calls=%fused_computation.3.clone.1 | loop fusion | flops 12581888 | bytes 16785408 | tf_op jit(solution)/shard_map/while/body/eval_jaxpr/while/body/eval_jaxpr/reduce_sum | solution.py:23
  217.8 0.1 dynamic_update_slice.33
  218.0 2.4 multiply_reduce_fusion.4
  220.4 5.7 %copy-done = f32[1024,4096]{1,0:T(8,128)} copy-done((f32[1024,4096]{1,0:T(8,128)}, f32[1024,4096]{1,0:T(8,128)S(1)}, u32[]{:S(2)}) %copy-start) | copy-done | bytes 16777240 | tf_op jit(solution)/shard_map/while/body/eval_jaxpr/while
  226.1 3.8 %fusion.63 = f32[4,1024,128]{2,1,0:T(8,128)} fusion(f32[4,1024,128]{2,1,0:T(8,128)} %get-tuple-element.173, s32[]{:T(128)} %get-tuple-element.170, bf16[4096,128]{1,0:T(8,128)(2,1)S(1)} %copy-done.3, f32[1024,4096]{1,0:T(8,128)S(1)} %get-tuple-element.160, f32[1024]{0:T(1024)S(1)} %get-tuple-element.159), kind=kOutput, calls=%fused_computation.6.clone.1 | convolution fusion | flops 1086324736 | bytes 18354688 | tf_op jit(solution)/shard_map/while/body/eval_jaxpr/while/body/eval_jaxpr/dot_general | solution.py:24
  229.9 8.6 %fusion.62 = f32[1024]{0:T(1024)S(1)} fusion(f32[1024,4096]{1,0:T(8,128)} %copy-done, f32[1024]{0:T(1024)S(1)} %get-tuple-element.159), kind=kLoop, calls=%fused_computation.3.clone.1 | loop fusion | flops 12581888 | bytes 16785408 | tf_op jit(solution)/shard_map/while/body/eval_jaxpr/while/body/eval_jaxpr/reduce_sum | solution.py:23
  238.6 0.1 dynamic_update_slice.33
  238.7 0.4 transpose_reshape.10
  239.2 1.0 reshape.249
  240.2 5.9 %all-to-all-start.2 = ((f32[32,1,128]{2,1,0:T(1,128)}), f32[32,1,128]{2,1,0:T(1,128)S(1)}, u32[]{:S(2)}, u32[]{:S(2)}) async-start(f32[32,1,128]{2,1,0:T(1,128)} %reshape.249), calls=%async_computation.2 | async-start | bytes 32768 | tf_op jit(solution)/shard_map/all_to_all | solution.py:103
  246.0 0.4 transpose_reshape.11
  246.5 1.0 reshape.251
  247.5 4.9 %all-to-all-done.2 = f32[32,1,128]{2,1,0:T(1,128)S(1)} async-done(((f32[32,1,128]{2,1,0:T(1,128)}), f32[32,1,128]{2,1,0:T(1,128)S(1)}, u32[]{:S(2)}, u32[]{:S(2)}) %all-to-all-start.2) | async-done | bytes 16416 | tf_op jit(solution)/shard_map/all_to_all | solution.py:103
  252.4 5.0 %all-to-all-start.5 = ((f32[32,1,128]{2,1,0:T(1,128)}), f32[32,1,128]{2,1,0:T(1,128)S(1)}, u32[]{:S(2)}, u32[]{:S(2)}) async-start(f32[32,1,128]{2,1,0:T(1,128)} %reshape.251), calls=%async_computation.5 | async-start | bytes 32768 | tf_op jit(solution)/shard_map/all_to_all | solution.py:104
  257.4 0.5 broadcast.126
  257.9 0.7 reduce.4
  258.6 0.4 reshape.250
  259.1 4.9 %all-to-all-done.5 = f32[32,1,128]{2,1,0:T(1,128)S(1)} async-done(((f32[32,1,128]{2,1,0:T(1,128)}), f32[32,1,128]{2,1,0:T(1,128)S(1)}, u32[]{:S(2)}, u32[]{:S(2)}) %all-to-all-start.5) | async-done | bytes 16416 | tf_op jit(solution)/shard_map/all_to_all | solution.py:104
  264.0 0.7 reduce.5
  264.7 0.4 reshape.252
  265.1 0.7 reduce_max.30
  265.8 1.0 multiply_reduce_fusion.2
  266.8 17.5 %all_to_all.88 = f32[8,2,1,8]{3,2,1,0:T(1,128)S(1)} all-to-all(f32[8,2,1,8]{3,2,1,0:T(1,128)S(1)} %bitcast.156), channel_id=1, replica_groups=mesh['prefix'=32,'sample'=8] {'sample'}, dimensions={0} | all-to-all | bytes 1024 | tf_op jit(solution)/shard_map/all_to_all | solution.py:118
  284.3 5.2 %all-to-all-start.1 = ((f32[256,2,1,8,128]{4,3,1,2,0:T(8,128)}), f32[256,2,1,8,128]{4,3,1,2,0:T(8,128)S(1)}, u32[]{:S(2)}, u32[]{:S(2)}) async-start(f32[256,2,1,8,128]{4,3,1,2,0:T(8,128)} %bitcast.6), calls=%async_computation.1 | async-start | bytes 4194304 | tf_op jit(solution)/shard_map/all_to_all | solution.py:102
  290.2 3.1 copy.113
  293.3 0.8 fusion.51
  294.1 0.2 fusion.38
  294.3 0.8 copy-done.1
  295.2 0.7 subtract_exponential_fusion.2
  295.9 40.3 %all-to-all-done.1 = f32[256,2,1,8,128]{4,3,1,2,0:T(8,128)S(1)} async-done(((f32[256,2,1,8,128]{4,3,1,2,0:T(8,128)}), f32[256,2,1,8,128]{4,3,1,2,0:T(8,128)S(1)}, u32[]{:S(2)}, u32[]{:S(2)}) %all-to-all-start.1) | async-done | bytes 2097184 | tf_op jit(solution)/shard_map/all_to_all | solution.py:102
  336.2 3.3 all-to-all-start.4
  339.6 1.3 multiply_reduce_fusion.1
  340.9 8.7 %all-to-all-done.4 = f32[8,2,1,8]{3,2,1,0:T(1,128)S(1)} async-done(((f32[8,2,1,8]{3,2,1,0:T(1,128)}), f32[8,2,1,8]{3,2,1,0:T(1,128)S(1)}, u32[]{:S(2)}, u32[]{:S(2)}) %all-to-all-start.4) | async-done | bytes 544 | tf_op jit(solution)/shard_map/all_to_all | solution.py:117
  349.6 3.3 all-to-all-start.3
  353.0 10.1 %all-to-all-done.3 = f32[8,2,1,8,128]{4,3,1,2,0:T(8,128)S(1)} async-done(((f32[8,2,1,8,128]{4,3,1,2,0:T(8,128)}), f32[8,2,1,8,128]{4,3,1,2,0:T(8,128)S(1)}, u32[]{:S(2)}, u32[]{:S(2)}) %all-to-all-start.3) | async-done | bytes 65568 | tf_op jit(solution)/shard_map/all_to_all | solution.py:116
  363.1 2.1 fusion.35
  365.2 0.6 convert_element_type.23
  (38 shorter events, 0.3 us)
Async XLA Ops:
  6.5 147.4 %all-gather.3.cloned.1.call-start = ((), (), s32[]{:S(2)}) async-start(), calls=%async_computation.7 | async-start | bytes 1081344 | tf_op jit(solution)/shard_map/all_gather | solution.py:83
  83.7 15.1 %copy-start.2 = (bf16[4096,1,256]{2,0,1:T(8,128)(2,1)S(1)}, bf16[4096,1,256]{2,0,1:T(8,128)(2,1)}, u32[]{:S(2)}) copy-start(bf16[4096,1,256]{2,0,1:T(8,128)(2,1)} %param.8) | copy-start | bytes 6291460
  155.7 8.1 %copy-start.3 = (bf16[4096,128]{1,0:T(8,128)(2,1)S(1)}, bf16[4096,128]{1,0:T(8,128)(2,1)}, u32[]{:S(2)}) copy-start(bf16[4096,128]{1,0:T(8,128)(2,1)} %get-tuple-element.185) | copy-start | bytes 3145732 | tf_op jit(solution)/shard_map/while/body/eval_jaxpr/while
  158.1 5.7 %copy-start = (f32[1024,4096]{1,0:T(8,128)}, f32[1024,4096]{1,0:T(8,128)S(1)}, u32[]{:S(2)}) copy-start(f32[1024,4096]{1,0:T(8,128)S(1)} %get-tuple-element.160) | copy-start | bytes 50331652 | tf_op jit(solution)/shard_map/while/body/eval_jaxpr/while
  176.4 8.1 %copy-start.3 = (bf16[4096,128]{1,0:T(8,128)(2,1)S(1)}, bf16[4096,128]{1,0:T(8,128)(2,1)}, u32[]{:S(2)}) copy-start(bf16[4096,128]{1,0:T(8,128)(2,1)} %get-tuple-element.185) | copy-start | bytes 3145732 | tf_op jit(solution)/shard_map/while/body/eval_jaxpr/while
  178.8 5.7 %copy-start = (f32[1024,4096]{1,0:T(8,128)}, f32[1024,4096]{1,0:T(8,128)S(1)}, u32[]{:S(2)}) copy-start(f32[1024,4096]{1,0:T(8,128)S(1)} %get-tuple-element.160) | copy-start | bytes 50331652 | tf_op jit(solution)/shard_map/while/body/eval_jaxpr/while
  197.2 8.1 %copy-start.3 = (bf16[4096,128]{1,0:T(8,128)(2,1)S(1)}, bf16[4096,128]{1,0:T(8,128)(2,1)}, u32[]{:S(2)}) copy-start(bf16[4096,128]{1,0:T(8,128)(2,1)} %get-tuple-element.185) | copy-start | bytes 3145732 | tf_op jit(solution)/shard_map/while/body/eval_jaxpr/while
  199.6 5.7 %copy-start = (f32[1024,4096]{1,0:T(8,128)}, f32[1024,4096]{1,0:T(8,128)S(1)}, u32[]{:S(2)}) copy-start(f32[1024,4096]{1,0:T(8,128)S(1)} %get-tuple-element.160) | copy-start | bytes 50331652 | tf_op jit(solution)/shard_map/while/body/eval_jaxpr/while
  218.0 8.1 %copy-start.3 = (bf16[4096,128]{1,0:T(8,128)(2,1)S(1)}, bf16[4096,128]{1,0:T(8,128)(2,1)}, u32[]{:S(2)}) copy-start(bf16[4096,128]{1,0:T(8,128)(2,1)} %get-tuple-element.185) | copy-start | bytes 3145732 | tf_op jit(solution)/shard_map/while/body/eval_jaxpr/while
  220.4 5.7 %copy-start = (f32[1024,4096]{1,0:T(8,128)}, f32[1024,4096]{1,0:T(8,128)S(1)}, u32[]{:S(2)}) copy-start(f32[1024,4096]{1,0:T(8,128)S(1)} %get-tuple-element.160) | copy-start | bytes 50331652 | tf_op jit(solution)/shard_map/while/body/eval_jaxpr/while
  240.2 12.2 %all-to-all-start.2 = ((f32[32,1,128]{2,1,0:T(1,128)}), f32[32,1,128]{2,1,0:T(1,128)S(1)}, u32[]{:S(2)}, u32[]{:S(2)}) async-start(f32[32,1,128]{2,1,0:T(1,128)} %reshape.249), calls=%async_computation.2 | async-start | bytes 32768 | tf_op jit(solution)/shard_map/all_to_all | solution.py:103
  252.4 11.6 %all-to-all-start.5 = ((f32[32,1,128]{2,1,0:T(1,128)}), f32[32,1,128]{2,1,0:T(1,128)S(1)}, u32[]{:S(2)}, u32[]{:S(2)}) async-start(f32[32,1,128]{2,1,0:T(1,128)} %reshape.251), calls=%async_computation.5 | async-start | bytes 32768 | tf_op jit(solution)/shard_map/all_to_all | solution.py:104
  284.3 51.9 %all-to-all-start.1 = ((f32[256,2,1,8,128]{4,3,1,2,0:T(8,128)}), f32[256,2,1,8,128]{4,3,1,2,0:T(8,128)S(1)}, u32[]{:S(2)}, u32[]{:S(2)}) async-start(f32[256,2,1,8,128]{4,3,1,2,0:T(8,128)} %bitcast.6), calls=%async_computation.1 | async-start | bytes 4194304 | tf_op jit(solution)/shard_map/all_to_all | solution.py:102
  290.1 3.1 copy-start.5
  290.1 3.2 copy-start.4
  293.2 1.9 copy-start.1
  336.2 13.4 %all-to-all-start.4 = ((f32[8,2,1,8]{3,2,1,0:T(1,128)}), f32[8,2,1,8]{3,2,1,0:T(1,128)S(1)}, u32[]{:S(2)}, u32[]{:S(2)}) async-start(f32[8,2,1,8]{3,2,1,0:T(1,128)} %bitcast.38), calls=%async_computation.4 | async-start | bytes 16384 | tf_op jit(solution)/shard_map/all_to_all | solution.py:117
  349.6 13.5 %all-to-all-start.3 = ((f32[8,2,1,8,128]{4,3,1,2,0:T(8,128)}), f32[8,2,1,8,128]{4,3,1,2,0:T(8,128)S(1)}, u32[]{:S(2)}, u32[]{:S(2)}) async-start(f32[8,2,1,8,128]{4,3,1,2,0:T(8,128)} %bitcast.10), calls=%async_computation.3 | async-start | bytes 131072 | tf_op jit(solution)/shard_map/all_to_all | solution.py:116
Sparse Core Ops, SparseCore 0:
  98.9 54.9 all-gather.2
where the time goes:
time: 377 us; the launch traced here: 373 us
  waiting for transfers between devices  123 us (33%)
  other arithmetic  85.1 us (23%)
  local copies, waits for them, and re-layouts  62 us (16%)
  blocking collectives  37.5 us (10%)
  matrix products  27.8 us (7%)
  starting transfers between devices  22.7 us (6%)
  between operations  14.3 us (4%)
    all_gather x1, waiting for transfers between devices, per_device(): everyone = lax.all_gather(own_heads, 'prefix', axis=0, tiled=True)  54 us
    unnamed x1, other arithmetic  45.2 us
    all_to_all x1, waiting for transfers between devices, per_device(): lax.all_to_all(numers, 'prefix', split_axis=0, concat_axis=0, tiled=True)  40.3 us
    reduce_sum x4, other arithmetic, one_block(): block_total = jnp.sum(weights, axis=1)  34.5 us
    unnamed x21, local copies, waits for them, and re-layouts  25 us
    while x16, local copies, waits for them, and re-layouts  22.9 us
    all_to_all x1, blocking collectives, per_device(): lax.all_to_all(queries, 'sample', split_axis=2, concat_axis=0, tiled=True)  20 us
    all_to_all x1, blocking collectives, per_device(): lax.all_to_all(head_total, 'sample', split_axis=0, concat_axis=2, tiled=T...  17.5 us
  transfers between devices with their start and end apart: 6, of which 6 were waited for; matrix products, arithmetic and copies ran while one was open for 3% of the time, Pallas kernels for 0%

commit v1 on v0

v1 whole, which is shorter than its diff:
```python
import functools
import math

import jax
import jax.numpy as jnp
from jax import lax
from jax.experimental import pallas as pl
from jax.experimental.pallas import tpu as pltpu
from jax.sharding import Mesh, PartitionSpec as P

F32 = jnp.float32
BF16 = jnp.bfloat16
LANES = 128
Y, ZL, CORE, X, ZH = 4, 4, 2, 4, 2
AXES = ("y", "zl", "core", "x", "zh")
WIDE = ("zl", "x", "zh")
STEP = 32000.0
FRACTION = 32767.0
MASKED = -1e30
VMEM = pl.BlockSpec(memory_space=pltpu.VMEM)
SMEM = pl.BlockSpec(memory_space=pltpu.SMEM)


def params(mib):
    return pltpu.CompilerParams(vmem_limit_bytes=mib * 2**20)


def lane_select(shape, columns):
    lane = lax.broadcasted_iota(jnp.int32, shape, 1)
    out = jnp.zeros(shape, F32)
    for i, column in enumerate(columns):
        out = jnp.where(lane == i, column, out)
    return out


def code(values):
    peak = jnp.maximum(jnp.max(jnp.abs(values), axis=1, keepdims=True), 1e-30)
    power = jnp.ceil(jnp.log2(peak))
    coded = jnp.round(values * (jnp.exp2(-power) * STEP))
    return coded.astype(jnp.int32).astype(jnp.int16), power


def split_weight(weight):
    whole = jnp.floor(weight * 0.5)
    return whole, jnp.round((weight - 2.0 * whole) * (0.5 * FRACTION))


def join_weight(whole, part):
    return 2.0 * whole + part * (2.0 / FRACTION)


def spread_kernel(q_ref, out_ref, rows_ref, *, copies):
    steps = q_ref.shape[1]
    tiles = q_ref.shape[2] // LANES
    for c in range(tiles):
        rows_ref[steps * c : steps * (c + 1), :] = q_ref[0, :, LANES * c : LANES * (c + 1)].astype(F32)
    rows = rows_ref[...].astype(BF16)
    for i in range(copies):
        out_ref[i] = rows


def spread(queries):
    count = queries.shape[1] * queries.shape[2] // LANES
    return pl.pallas_call(
        functools.partial(spread_kernel, copies=ZL),
        out_shape=jax.ShapeDtypeStruct((ZL, count, LANES), BF16),
        in_specs=[VMEM],
        out_specs=VMEM,
        scratch_shapes=[pltpu.VMEM((count, LANES), F32)],
        compiler_params=params(16),
        name="spread",
    )(queries)


def local_kernel(len_ref, q_ref, kv_ref, new_ref, numer_ref, stat_ref, s_ref, new_pad, *, heads, chunk, factor):
    rows = q_ref.shape[1]
    group = rows // heads
    total = kv_ref.shape[0]
    news = new_ref.shape[0]
    q = q_ref[0]
    lane = lax.broadcasted_iota(jnp.int32, (rows, chunk), 1)
    row = lax.broadcasted_iota(jnp.int32, (rows, chunk), 0)
    own = (lane % heads) == (row // group)
    limit = jnp.where(own, lane, total)
    used = len_ref[0] * heads
    peak = None
    for j in range(total // chunk):
        s = lax.dot_general(
            q, kv_ref[j * chunk : (j + 1) * chunk, :LANES], (((1,), (1,)), ((), ())), preferred_element_type=F32
        )
        s = jnp.where(limit < used - j * chunk, s, MASKED)
        s_ref[:, j * chunk : (j + 1) * chunk] = s
        for i in range(chunk // LANES):
            part = s[:, i * LANES : (i + 1) * LANES]
            peak = part if peak is None else jnp.maximum(peak, part)
    new_pad[...] = jnp.zeros_like(new_pad)
    new_pad[:news, :] = new_ref[...]
    s_new = lax.dot_general(q, new_pad[:, :LANES], (((1,), (1,)), ((), ())), preferred_element_type=F32)
    steps = news // heads
    lane = lane[:, :LANES]
    row = row[:, :LANES]
    valid = own[:, :LANES] & (lane // heads <= row % steps)
    s_new = jnp.where(valid, s_new, MASKED)
    peak = jnp.max(jnp.maximum(peak, s_new), axis=1, keepdims=True)
    p_new = jnp.exp2((s_new - peak) * factor)
    weight = p_new
    numer = jnp.dot(p_new.astype(BF16), new_pad[:, LANES:], preferred_element_type=F32)
    for j in range(total // chunk):
        p = jnp.exp2((s_ref[:, j * chunk : (j + 1) * chunk] - peak) * factor)
        for i in range(chunk // LANES):
            weight = weight + p[:, i * LANES : (i + 1) * LANES]
        numer = numer + jnp.dot(
            p.astype(BF16), kv_ref[j * chunk : (j + 1) * chunk, LANES:], preferred_element_type=F32
        )
    numer_ref[...] = numer
    scale = factor / math.log2(math.e)
    stat_ref[...] = lane_select((rows, LANES), (peak * scale, jnp.sum(weight, axis=1, keepdims=True)))


def local(lengths, rows, cache, new, heads, factor):
    count = rows.shape[1]
    return pl.pallas_call(
        functools.partial(local_kernel, heads=heads, chunk=512, factor=factor),
        out_shape=(jax.ShapeDtypeStruct((count, LANES), F32), jax.ShapeDtypeStruct((count, LANES), F32)),
        in_specs=[SMEM, VMEM, VMEM, VMEM],
        out_specs=(VMEM, VMEM),
        scratch_shapes=[pltpu.VMEM((count, cache.shape[0]), F32), pltpu.VMEM((LANES, 2 * LANES), BF16)],
        compiler_params=params(32),
        name="local",
    )(lengths, rows, cache, new)


def document_kernel(q_ref, kv0_ref, kv1_ref, out_ref, s0_ref, s1_ref, *, tile, chunk, factor):
    rows = q_ref.shape[0]
    kv = (kv0_ref, kv1_ref)
    held = (s0_ref, s1_ref)
    pieces = kv0_ref.shape[0] // chunk
    units = [(r, b) for r in range(rows // tile) for b in range(2)]
    scale = factor / math.log2(math.e)

    def scores(u, j):
        r, b = units[u]
        s = lax.dot_general(
            q_ref[r * tile : (r + 1) * tile, :],
            kv[b][j * chunk : (j + 1) * chunk, :LANES],
            (((1,), (1,)), ((), ())),
            preferred_element_type=F32,
        )
        held[u % 2][:, j * chunk : (j + 1) * chunk] = s
        peak = s[:, :LANES]
        for i in range(1, chunk // LANES):
            peak = jnp.maximum(peak, s[:, i * LANES : (i + 1) * LANES])
        return peak

    running = None
    for j in range(pieces):
        part = scores(0, j)
        running = part if running is None else jnp.maximum(running, part)
    done = []
    stats = []
    for u, (r, b) in enumerate(units):
        peak = jnp.max(running, axis=1, keepdims=True)
        running = total = numer = None
        for j in range(pieces):
            if u + 1 < len(units):
                part = scores(u + 1, j)
                running = part if running is None else jnp.maximum(running, part)
            p = jnp.exp2((held[u % 2][:, j * chunk : (j + 1) * chunk] - peak) * factor)
            for i in range(chunk // LANES):
                part = p[:, i * LANES : (i + 1) * LANES]
                total = part if total is None else total + part
            part = jnp.dot(
                p.astype(BF16), kv[b][j * chunk : (j + 1) * chunk, LANES:], preferred_element_type=F32
            )
            numer = part if numer is None else numer + part
        done.append((peak, jnp.sum(total, axis=1, keepdims=True), numer))
        if b == 1:
            (peak0, total0, numer0), (peak1, total1, numer1) = done
            done = []
            top = jnp.maximum(peak0, peak1) * scale
            base = jnp.round(top * 2.0)
            factor0 = jnp.exp(peak0 * scale - base * 0.5)
            factor1 = jnp.exp(peak1 * scale - base * 0.5)
            coded, power = code(numer0 * factor0 + numer1 * factor1)
            out_ref[r * tile : (r + 1) * tile, :] = coded
            whole, part = split_weight(total0 * factor0 + total1 * factor1)
            for i in range(tile // LANES):
                at = slice(i * LANES, (i + 1) * LANES)
                stats.append((base[at], whole[at], part[at], power[at]))
    blocks = len(stats)
    columns = [stats[i][j] for j in range(4) for i in range(blocks)]
    across = jnp.transpose(lane_select((LANES, LANES), columns))
    out_ref[rows : rows + 16, :] = across[:16].astype(jnp.int32).astype(jnp.int16)


def document(rows, kv0, kv1, factor):
    count = rows.shape[0]
    tile = 256
    return pl.pallas_call(
        functools.partial(document_kernel, tile=tile, chunk=512, factor=factor),
        out_shape=jax.ShapeDtypeStruct((count + 16, LANES), jnp.int16),
        in_specs=[VMEM, VMEM, VMEM],
        out_specs=VMEM,
        scratch_shapes=[pltpu.VMEM((tile, kv0.shape[0]), F32)] * 2,
        compiler_params=params(40),
        name="document",
    )(rows, kv0, kv1)


def merge_kernel(*refs):
    parts, out_ref = refs[:-1], refs[-1]
    blocks = 4
    rows = parts[0].shape[0] - 16
    stats = [p[rows : rows + 16, :].astype(jnp.int32).astype(F32) for p in parts]
    tops = [s[0:blocks] for s in stats]
    top = functools.reduce(jnp.maximum, tops)
    shrink = [jnp.exp((t - top) * 0.5) for t in tops]
    weight = sum(
        f * join_weight(s[blocks : 2 * blocks], s[2 * blocks : 3 * blocks]) for f, s in zip(shrink, stats)
    )
    whole, part = split_weight(weight)
    scales = [f * (jnp.exp2(s[3 * blocks : 4 * blocks]) / STEP) for f, s in zip(shrink, stats)]
    used = blocks * (3 + len(parts))
    across = jnp.concatenate([top, whole, part] + scales + [jnp.zeros((LANES - used, LANES), F32)], axis=0)
    down = jnp.transpose(across)
    owners = LANES // 16
    for b in range(blocks):
        numer = None
        for i, p in enumerate(parts):
            at = 4 * (3 + i) + b
            term = p[b * LANES : (b + 1) * LANES, :].astype(jnp.int32).astype(F32) * down[:, at : at + 1]
            numer = term if numer is None else numer + term
        coded, power = code(numer)
        columns = [down[:, blocks * j + b : blocks * j + b + 1] for j in range(3)] + [power]
        tile = lane_select((LANES, LANES), columns).astype(jnp.int32).astype(jnp.int16)
        for s in range(owners):
            out_ref[b * owners + s, 0:16, :] = coded[16 * s : 16 * (s + 1), :]
            out_ref[b * owners + s, 16:32, :] = tile[16 * s : 16 * (s + 1), :]


def merge(parts):
    return pl.pallas_call(
        merge_kernel,
        out_shape=jax.ShapeDtypeStruct((32, 32, LANES), jnp.int16),
        in_specs=[VMEM] * len(parts),
        out_specs=VMEM,
        compiler_params=params(32),
        name="merge",
    )(*parts)


def finish_kernel(got_ref, numer_ref, stat_ref, out_ref, rows_ref, *, heads):
    steps = out_ref.shape[1]
    group = numer_ref.shape[0] // heads
    for k in range(heads):
        at = slice(k * group, (k + 1) * group)
        peak = stat_ref[at, 0:1]
        tiles = [got_ref[z * heads + k, 16:32, :].astype(jnp.int32).astype(F32) for z in range(ZL)]
        tops = [t[:, 0:1] * 0.5 for t in tiles]
        top = functools.reduce(jnp.maximum, tops, peak)
        shrink = jnp.exp(peak - top)
        numer = numer_ref[at, :] * shrink
        weight = stat_ref[at, 1:2] * shrink
        for z in range(ZL):
            shrink = jnp.exp(tops[z] - top)
            weight = weight + shrink * join_weight(tiles[z][:, 1:2], tiles[z][:, 2:3])
            coded = got_ref[z * heads + k, 0:16, :].astype(jnp.int32).astype(F32)
            numer = numer + coded * (shrink * (jnp.exp2(tiles[z][:, 3:4]) / STEP))
        rows_ref[at, :] = numer / weight
    for c in range(out_ref.shape[2] // LANES):
        out_ref[0, :, LANES * c : LANES * (c + 1)] = rows_ref[steps * c : steps * (c + 1), :].astype(BF16)


def finish(got, numer, stat, shape, heads):
    return pl.pallas_call(
        functools.partial(finish_kernel, heads=heads),
        out_shape=jax.ShapeDtypeStruct(shape, BF16),
        in_specs=[VMEM] * 3,
        out_specs=VMEM,
        scratch_shapes=[pltpu.VMEM(numer.shape, F32)],
        compiler_params=params(16),
        name="finish",
    )(got, numer, stat)


def per_device(queries, prefix_kv, suffix_kv, new_kv, lengths):
    positions, _, width = prefix_kv.shape
    head_dim = width // 2
    heads = suffix_kv.shape[2]
    factor = math.log2(math.e) / math.sqrt(head_dim)
    kv_own = prefix_kv.reshape(positions, width)
    kv_other = lax.ppermute(kv_own, "core", [(0, 1), (1, 0)])
    spread_rows = spread(queries)
    gathered = lax.all_to_all(
        spread_rows.reshape(ZL * heads, 16, LANES), WIDE, split_axis=0, concat_axis=0, tiled=True
    ).reshape(-1, LANES)
    cache = suffix_kv.reshape(-1, width)
    numer, stat = local(lengths, spread_rows, cache, new_kv.reshape(-1, width), heads, factor)
    others = [lax.ppermute(gathered, "y", [(j, (j - d) % Y) for j in range(Y)]) for d in (1, 3, 2)]
    parts = [document(gathered, kv_own, kv_other, factor)]
    for d, rows in zip((1, 3, 2), others):
        part = document(rows, kv_own, kv_other, factor)
        parts.append(lax.ppermute(part, "y", [(j, (j + d) % Y) for j in range(Y)]))
    merged = merge(parts)
    got = lax.all_to_all(merged, WIDE, split_axis=0, concat_axis=0, tiled=True)
    return finish(got, numer, stat, queries.shape, heads)


def solution(mesh):
    devices = mesh.devices.reshape(Y, ZL, CORE, X, ZH)
    fine = Mesh(devices, AXES)
    prefix, sample = ("y", "zl", "core"), ("x", "zh")
    owner = P(prefix + sample)
    in_specs = (owner, P(prefix, sample), owner, owner, owner)
    return jax.shard_map(per_device, mesh=fine, in_specs=in_specs, out_specs=owner, check_vma=False)
```

time: 377 us -> 81.6 us (0.22); the launches traced: 373 us -> 81.3 us
  waiting for transfers between devices: 123 us -> 6.55 us
  other arithmetic: 85.1 us -> 0 us
  local copies, waits for them, and re-layouts: 62 us -> 4.54 us
  Pallas kernels: 0 us -> 31.5 us
  matrix products: 27.8 us -> 0 us
  blocking collectives: 37.5 us -> 21.5 us
  between operations: 14.3 us -> 0.71 us
  starting transfers between devices: 22.7 us -> 16.4 us
    all_to_all x5 -> x1, waiting for transfers between devices: 69 us -> 6.16 us  [per_device(): got = lax.all_to_all(merged, WIDE, split_axis=0, concat_axis=0, tiled=True)]
    all_gather x1 -> x0, waiting for transfers between devices: 54 us -> none  [per_device(): everyone = lax.all_gather(own_heads, 'prefix', axis=0, tiled=True)]
    unnamed x1 -> x0, other arithmetic: 45.2 us -> none
    reduce_sum x7 -> x0, other arithmetic: 37 us -> none  [the longest x4 34.5 us: one_block(): block_total = jnp.sum(weights, axis=1)]
    pallas_call x0 -> x8, Pallas kernels: none -> 31.5 us  [the longest x4 23.5 us: document(): pl.pallas_call(functools.partial(document_kernel, tile=tile, chunk=512, f...]
    dot_general x10 -> x0, matrix products: 27.8 us -> none  [the longest x4 15.3 us: one_block(): jnp.dot(weights.astype(jnp.bfloat16), values_part, preferred_element_type...]
    while x16 -> x0, local copies, waits for them, and re-layouts: 22.9 us -> none
    unnamed x21 -> x10, local copies, waits for them, and re-layouts: 25 us -> 4.54 us
  transfers between devices with their start and end apart: 6 -> 8, of which waited for: 6 -> 2; matrix products, arithmetic and copies ran while one was open for 3% -> 0% of each run, Pallas kernels for 0% -> 32%
where the time goes in v1:
time: 81.6 us; the launch traced here: 81.3 us
  Pallas kernels  31.5 us (39%)
  blocking collectives  21.5 us (26%)
  starting transfers between devices  16.4 us (20%)
  waiting for transfers between devices  6.55 us (8%)
  local copies, waits for them, and re-layouts  4.54 us (6%)
    pallas_call x4, Pallas kernels, document(): pl.pallas_call(functools.partial(document_kernel, tile=tile, chunk=512, f...  23.5 us
    all_to_all x1, blocking collectives, per_device(): lax.all_to_all(spread_rows.reshape(ZL * heads, 16, LANES), WIDE, split_ax...  21.5 us
    ppermute x3, starting transfers between devices, per_device(): parts.append(lax.ppermute(part, 'y', [(j, (j + d) % Y) for j in range(Y)]))  7.06 us
    all_to_all x1, waiting for transfers between devices, per_device(): got = lax.all_to_all(merged, WIDE, split_axis=0, concat_axis=0, tiled=True)  6.16 us
    ppermute x3, starting transfers between devices, per_device(): lax.ppermute(gathered, 'y', [(j, (j - d) % Y) for j in range(Y)])  5.22 us
    unnamed x10, local copies, waits for them, and re-layouts  4.54 us
    all_to_all x1, starting transfers between devices, per_device(): got = lax.all_to_all(merged, WIDE, split_axis=0, concat_axis=0, tiled=True)  4.15 us
    pallas_call x1, Pallas kernels, finish(): pl.pallas_call(functools.partial(finish_kernel, heads=heads), out_shape=j...  3.96 us
  transfers between devices with their start and end apart: 8, of which 2 were waited for; matrix products, arithmetic and copies ran while one was open for 0% of the time, Pallas kernels for 32%

profile of v1, /device:TPU:32, one launch (start us, length us, event | category | flops | bytes accessed | tf_op | source)
XLA Modules:
  0.0 81.3 jit_solution(8755724282058080300)
XLA Ops:
  0.0 0.0 collective-permute-start
  0.0 0.0 copy-start.3
  0.0 0.8 copy-done.3
  0.8 21.5 %all_to_all.10 = bf16[32,16,128]{2,1,0:T(8,128)(2,1)S(1)} all-to-all(bf16[32,16,128]{2,1,0:T(8,128)(2,1)S(1)} %bitcast.11), channel_id=1, replica_groups=mesh['y'=4,'zl'=4,'core'=2,'x'=4,'zh'=2] {'zl','x','zh'}, dimensions={0} | all-to-all | bytes 262144 | tf_op jit(solution)/shard_map/all_to_all | solution.py:294
  22.3 3.0 %collective-permute-start.1 = (bf16[512,128]{1,0:T(8,128)(2,1)S(1)}, bf16[512,128]{1,0:T(8,128)(2,1)S(1)}, u32[]{:S(2)}, u32[]{:S(2)}) collective-permute-start(bf16[512,128]{1,0:T(8,128)(2,1)S(1)} %bitcast.12), channel_id=1, source_target_pairs={{0,192},{64,0},{128,64},{192,128},{1,193},{65,1},{129,65},{193,129... | collective-permute-start | bytes 393224 | tf_op jit(solution)/shard_map/ppermute | solution.py:299
  25.3 0.0 collective-permute-start.3
  25.3 2.2 %collective-permute-start.5 = (bf16[512,128]{1,0:T(8,128)(2,1)S(1)}, bf16[512,128]{1,0:T(8,128)(2,1)S(1)}, u32[]{:S(2)}, u32[]{:S(2)}) collective-permute-start(bf16[512,128]{1,0:T(8,128)(2,1)S(1)} %bitcast.14), channel_id=1, source_target_pairs={{0,128},{64,192},{128,0},{192,64},{1,129},{65,193},{129,1},{193,65... | collective-permute-start | bytes 393224 | tf_op jit(solution)/shard_map/ppermute | solution.py:299
  27.5 0.4 collective-permute-done.1.q_ref
  27.9 0.0 collective-permute-done.kv1_ref
  27.9 0.0 copy-start
  27.9 1.6 %copy-done = bf16[4096,1,256]{2,0,1:T(8,128)(2,1)S(1)} copy-done((bf16[4096,1,256]{2,0,1:T(8,128)(2,1)S(1)}, bf16[4096,1,256]{2,0,1:T(8,128)(2,1)}, u32[]{:S(2)}) %copy-start) | copy-done | bytes 2097176
  29.5 5.9 %document.5 = s16[528,128]{1,0:T(8,128)(2,1)S(1)} custom-call(bf16[512,128]{1,0:T(8,128)(2,1)S(1)} %collective-permute-done.1.q_ref, bf16[4096,256]{1,0:T(8,128)(2,1)S(1)} %bitcast.6, bf16[4096,256]{1,0:T(8,128)(2,1)S(1)} %collective-permute-done.kv1_ref), custom_call_target="tpu_custom_call" | custom-call | tf_op jit(solution)/shard_map/document/pallas_call | solution.py:199
  35.4 1.7 %collective-permute-start.2 = (s16[528,128]{1,0:T(8,128)(2,1)S(1)}, s16[528,128]{1,0:T(8,128)(2,1)S(1)}, u32[]{:S(2)}, u32[]{:S(2)}) collective-permute-start(s16[528,128]{1,0:T(8,128)(2,1)S(1)} %document.5), channel_id=1, source_target_pairs={{0,64},{64,128},{128,192},{192,0},{1,65},{65,129},{129,193},{193,1... | collective-permute-start | bytes 405512 | tf_op jit(solution)/shard_map/ppermute | solution.py:303
  37.1 0.0 collective-permute-done.3.q_ref
  37.1 5.9 %document.6 = s16[528,128]{1,0:T(8,128)(2,1)S(1)} custom-call(bf16[512,128]{1,0:T(8,128)(2,1)S(1)} %collective-permute-done.3.q_ref, bf16[4096,256]{1,0:T(8,128)(2,1)S(1)} %bitcast.7, bf16[4096,256]{1,0:T(8,128)(2,1)S(1)} %collective-permute-done.kv1_ref), custom_call_target="tpu_custom_call" | custom-call | tf_op jit(solution)/shard_map/document/pallas_call | solution.py:199
  43.0 0.0 copy-start.1
  43.0 3.6 %collective-permute-start.4 = (s16[528,128]{1,0:T(8,128)(2,1)S(1)}, s16[528,128]{1,0:T(8,128)(2,1)S(1)}, u32[]{:S(2)}, u32[]{:S(2)}) collective-permute-start(s16[528,128]{1,0:T(8,128)(2,1)S(1)} %document.6), channel_id=1, source_target_pairs={{0,192},{64,0},{128,64},{192,128},{1,193},{65,1},{129,65},{193,129... | collective-permute-start | bytes 405512 | tf_op jit(solution)/shard_map/ppermute | solution.py:303
  46.6 0.0 collective-permute-done.5.q_ref
  46.6 5.8 %document.7 = s16[528,128]{1,0:T(8,128)(2,1)S(1)} custom-call(bf16[512,128]{1,0:T(8,128)(2,1)S(1)} %collective-permute-done.5.q_ref, bf16[4096,256]{1,0:T(8,128)(2,1)S(1)} %bitcast.8, bf16[4096,256]{1,0:T(8,128)(2,1)S(1)} %collective-permute-done.kv1_ref), custom_call_target="tpu_custom_call" | custom-call | tf_op jit(solution)/shard_map/document/pallas_call | solution.py:199
  52.4 0.0 copy-start.4
  52.4 1.8 %collective-permute-start.6 = (s16[528,128]{1,0:T(8,128)(2,1)S(1)}, s16[528,128]{1,0:T(8,128)(2,1)S(1)}, u32[]{:S(2)}, u32[]{:S(2)}) collective-permute-start(s16[528,128]{1,0:T(8,128)(2,1)S(1)} %document.7), channel_id=1, source_target_pairs={{0,128},{64,192},{128,0},{192,64},{1,129},{65,193},{129,1},{193,65... | collective-permute-start | bytes 405512 | tf_op jit(solution)/shard_map/ppermute | solution.py:303
  54.1 0.0 copy-done.1
  54.1 5.9 %document.4.refs_0_ = s16[528,128]{1,0:T(8,128)(2,1)S(1)} custom-call(bf16[512,128]{1,0:T(8,128)(2,1)S(1)} %bitcast.15, bf16[4096,256]{1,0:T(8,128)(2,1)S(1)} %bitcast.9, bf16[4096,256]{1,0:T(8,128)(2,1)S(1)} %collective-permute-done.kv1_ref), custom_call_target="tpu_custom_call" | custom-call | tf_op jit(solution)/shard_map/document/pallas_call | solution.py:199
  60.1 0.0 collective-permute-done.2.refs_1_
  60.1 0.0 collective-permute-done.4.refs_2_
  60.1 0.0 collective-permute-done.6.refs_3_
  60.1 1.8 %merge.1 = s16[32,32,128]{2,1,0:T(8,128)(2,1)} custom-call(s16[528,128]{1,0:T(8,128)(2,1)S(1)} %document.4.refs_0_, s16[528,128]{1,0:T(8,128)(2,1)S(1)} %collective-permute-done.2.refs_1_, s16[528,128]{1,0:T(8,128)(2,1)S(1)} %collective-permute-done.4.refs_2_, s16[528,128]{1,0:T(8,128)(2,1)S(1)} %collective-permute-done.6.refs_3_), custom_call_target="tpu_custom_call" | custom-call | tf_op jit(solution)/shard_map/merge/pallas_call | solution.py:242
  61.9 4.2 %all-to-all-start.1 = ((s16[32,32,128]{2,1,0:T(8,128)(2,1)}), s16[32,32,128]{2,1,0:T(8,128)(2,1)S(1)}, u32[]{:S(2)}, u32[]{:S(2)}) async-start(s16[32,32,128]{2,1,0:T(8,128)(2,1)} %merge.1), calls=%async_computation.1 | async-start | bytes 524288 | tf_op jit(solution)/shard_map/all_to_all | solution.py:305
  66.8 0.0 copy-done.4
  66.8 0.0 copy-start.2
  66.8 2.2 %copy-done.2 = bf16[1,1024,8,256]{3,2,1,0:T(8,128)(2,1)S(1)} copy-done((bf16[1,1024,8,256]{3,2,1,0:T(8,128)(2,1)S(1)}, bf16[1,1024,8,256]{3,2,1,0:T(8,128)(2,1)}, u32[]{:S(2)}) %copy-start.2) | copy-done | bytes 4194328
  69.0 2.2 %local.1 = (f32[128,128]{1,0:T(8,128)S(1)}, f32[128,128]{1,0:T(8,128)S(1)}) custom-call(s32[1]{0:T(128)S(6)} %copy.6.len_ref, bf16[4,128,128]{2,1,0:T(8,128)(2,1)S(1)} %spread.1.q_ref, bf16[8192,256]{1,0:T(8,128)(2,1)S(1)} %bitcast.10, bf16[16,256]{1,0:T(8,128)(2,1)S(1)} %bitcast.16), custom_call_target="tpu_custom_call" | custom-call | tf_op jit(solution)/shard_map/local/pallas_call | solution.py:122
  71.2 6.2 %all-to-all-done.1.got_ref = s16[32,32,128]{2,1,0:T(8,128)(2,1)S(1)} async-done(((s16[32,32,128]{2,1,0:T(8,128)(2,1)}), s16[32,32,128]{2,1,0:T(8,128)(2,1)S(1)}, u32[]{:S(2)}, u32[]{:S(2)}) %all-to-all-start.1) | async-done | bytes 262176 | tf_op jit(solution)/shard_map/all_to_all | solution.py:305
  77.3 4.0 %finish.1 = bf16[1,2,8192]{2,1,0:T(2,128)(2,1)} custom-call(s16[32,32,128]{2,1,0:T(8,128)(2,1)S(1)} %all-to-all-done.1.got_ref, f32[128,128]{1,0:T(8,128)S(1)} %get-tuple-element.7.numer_ref, f32[128,128]{1,0:T(8,128)S(1)} %get-tuple-element.8.stat_ref), custom_call_target="tpu_custom_call" | custom-call | tf_op jit(solution)/shard_map/finish/pallas_call | solution.py:275
  (1 shorter events, 0.0 us)
Async XLA Ops:
  0.0 27.9 %collective-permute-start = (bf16[4096,256]{1,0:T(8,128)(2,1)}, bf16[4096,256]{1,0:T(8,128)(2,1)S(1)}, u32[]{:S(2)}, u32[]{:S(2)}) collective-permute-start(bf16[4096,256]{1,0:T(8,128)(2,1)} %bitcast.5), channel_id=1, source_target_pairs={{0,8},{8,0},{1,9},{9,1},{2,10},{10,2},{3,11},{11,3},{4,12},{12,4},... | collective-permute-start | bytes 6291464 | tf_op jit(solution)/shard_map/ppermute | solution.py:292
  0.0 0.8 copy-start.3
  22.3 5.6 %collective-permute-start.1 = (bf16[512,128]{1,0:T(8,128)(2,1)S(1)}, bf16[512,128]{1,0:T(8,128)(2,1)S(1)}, u32[]{:S(2)}, u32[]{:S(2)}) collective-permute-start(bf16[512,128]{1,0:T(8,128)(2,1)S(1)} %bitcast.12), channel_id=1, source_target_pairs={{0,192},{64,0},{128,64},{192,128},{1,193},{65,1},{129,65},{193,129... | collective-permute-start | bytes 393224 | tf_op jit(solution)/shard_map/ppermute | solution.py:299
  25.3 11.8 %collective-permute-start.3 = (bf16[512,128]{1,0:T(8,128)(2,1)S(1)}, bf16[512,128]{1,0:T(8,128)(2,1)S(1)}, u32[]{:S(2)}, u32[]{:S(2)}) collective-permute-start(bf16[512,128]{1,0:T(8,128)(2,1)S(1)} %bitcast.13), channel_id=1, source_target_pairs={{0,64},{64,128},{128,192},{192,0},{1,65},{65,129},{129,193},{193,1... | collective-permute-start | bytes 393224 | tf_op jit(solution)/shard_map/ppermute | solution.py:299
  25.3 21.2 %collective-permute-start.5 = (bf16[512,128]{1,0:T(8,128)(2,1)S(1)}, bf16[512,128]{1,0:T(8,128)(2,1)S(1)}, u32[]{:S(2)}, u32[]{:S(2)}) collective-permute-start(bf16[512,128]{1,0:T(8,128)(2,1)S(1)} %bitcast.14), channel_id=1, source_target_pairs={{0,128},{64,192},{128,0},{192,64},{1,129},{65,193},{129,1},{193,65... | collective-permute-start | bytes 393224 | tf_op jit(solution)/shard_map/ppermute | solution.py:299
  27.9 1.6 %copy-start = (bf16[4096,1,256]{2,0,1:T(8,128)(2,1)S(1)}, bf16[4096,1,256]{2,0,1:T(8,128)(2,1)}, u32[]{:S(2)}) copy-start(bf16[4096,1,256]{2,0,1:T(8,128)(2,1)} %param.6) | copy-start | bytes 6291460
  35.4 24.7 %collective-permute-start.2 = (s16[528,128]{1,0:T(8,128)(2,1)S(1)}, s16[528,128]{1,0:T(8,128)(2,1)S(1)}, u32[]{:S(2)}, u32[]{:S(2)}) collective-permute-start(s16[528,128]{1,0:T(8,128)(2,1)S(1)} %document.5), channel_id=1, source_target_pairs={{0,64},{64,128},{128,192},{192,0},{1,65},{65,129},{129,193},{193,1... | collective-permute-start | bytes 405512 | tf_op jit(solution)/shard_map/ppermute | solution.py:303
  43.0 11.1 %copy-start.1 = (bf16[4096,1,256]{2,0,1:T(8,128)(2,1)S(1)}, bf16[4096,1,256]{2,0,1:T(8,128)(2,1)}, u32[]{:S(2)}) copy-start(bf16[4096,1,256]{2,0,1:T(8,128)(2,1)} %param.6) | copy-start | bytes 6291460
  43.0 17.1 %collective-permute-start.4 = (s16[528,128]{1,0:T(8,128)(2,1)S(1)}, s16[528,128]{1,0:T(8,128)(2,1)S(1)}, u32[]{:S(2)}, u32[]{:S(2)}) collective-permute-start(s16[528,128]{1,0:T(8,128)(2,1)S(1)} %document.6), channel_id=1, source_target_pairs={{0,192},{64,0},{128,64},{192,128},{1,193},{65,1},{129,65},{193,129... | collective-permute-start | bytes 405512 | tf_op jit(solution)/shard_map/ppermute | solution.py:303
  52.4 14.4 %copy-start.4 = (bf16[1,2,8,256]{3,2,1,0:T(8,128)(2,1)S(1)}, bf16[1,2,8,256]{3,2,1,0:T(8,128)(2,1)}, u32[]{:S(2)}) copy-start(bf16[1,2,8,256]{3,2,1,0:T(8,128)(2,1)} %param.8) | copy-start | bytes 24580
  52.4 7.7 %collective-permute-start.6 = (s16[528,128]{1,0:T(8,128)(2,1)S(1)}, s16[528,128]{1,0:T(8,128)(2,1)S(1)}, u32[]{:S(2)}, u32[]{:S(2)}) collective-permute-start(s16[528,128]{1,0:T(8,128)(2,1)S(1)} %document.7), channel_id=1, source_target_pairs={{0,128},{64,192},{128,0},{192,64},{1,129},{65,193},{129,1},{193,65... | collective-permute-start | bytes 405512 | tf_op jit(solution)/shard_map/ppermute | solution.py:303
  61.9 15.4 %all-to-all-start.1 = ((s16[32,32,128]{2,1,0:T(8,128)(2,1)}), s16[32,32,128]{2,1,0:T(8,128)(2,1)S(1)}, u32[]{:S(2)}, u32[]{:S(2)}) async-start(s16[32,32,128]{2,1,0:T(8,128)(2,1)} %merge.1), calls=%async_computation.1 | async-start | bytes 524288 | tf_op jit(solution)/shard_map/all_to_all | solution.py:305
  66.8 2.2 %copy-start.2 = (bf16[1,1024,8,256]{3,2,1,0:T(8,128)(2,1)S(1)}, bf16[1,1024,8,256]{3,2,1,0:T(8,128)(2,1)}, u32[]{:S(2)}) copy-start(bf16[1,1024,8,256]{3,2,1,0:T(8,128)(2,1)} %param.7) | copy-start | bytes 12582916

commit v2 on v1

v2 whole, which is shorter than its diff:
```python
import functools
import math

import jax
import jax.numpy as jnp
from jax import lax
from jax.experimental import pallas as pl
from jax.experimental.pallas import tpu as pltpu
from jax.sharding import Mesh, PartitionSpec as P

F32 = jnp.float32
BF16 = jnp.bfloat16
LANES = 128
Y, ZL, CORE, X, ZH = 4, 4, 2, 4, 2
AXES = ("y", "zl", "core", "x", "zh")
WIDE = ("zl", "x", "zh")
BITS = 14.9
FRACTION = 32767.0
MASKED = -1e30
VMEM = pl.BlockSpec(memory_space=pltpu.VMEM)
HBM = pl.BlockSpec(memory_space=pltpu.HBM)
SMEM = pl.BlockSpec(memory_space=pltpu.SMEM)


def params(mib):
    return pltpu.CompilerParams(vmem_limit_bytes=mib * 2**20)


def lane_select(shape, columns):
    lane = lax.broadcasted_iota(jnp.int32, shape, 1)
    out = jnp.zeros(shape, F32)
    for i, column in enumerate(columns):
        out = jnp.where(lane == i, column, out)
    return out


def toward_zero(values):
    return values.astype(jnp.int32).astype(F32)


def code(values):
    peak = jnp.maximum(jnp.max(jnp.abs(values), axis=1, keepdims=True), 1e-30)
    power = toward_zero(jnp.log2(peak) + 129.0) - 128.0
    coded = jnp.round(values * jnp.exp2(BITS - power))
    return coded.astype(jnp.int32).astype(jnp.int16), power


def split_weight(weight):
    whole = toward_zero(weight * 0.5)
    return whole, weight * (0.5 * FRACTION) - whole * FRACTION


def join_weight(whole, part):
    return 2.0 * whole + part * (2.0 / FRACTION)


def spread_kernel(q_ref, out_ref, held_ref, rows_ref, sem, *, copies):
    copy = pltpu.make_async_copy(q_ref, held_ref, sem)
    copy.start()
    copy.wait()
    steps = q_ref.shape[1]
    tiles = q_ref.shape[2] // LANES
    for c in range(tiles):
        rows_ref[steps * c : steps * (c + 1), :] = held_ref[0, :, LANES * c : LANES * (c + 1)].astype(F32)
    rows = rows_ref[...].astype(BF16)
    for i in range(copies):
        out_ref[i] = rows


def spread(queries):
    count = queries.shape[1] * queries.shape[2] // LANES
    return pl.pallas_call(
        functools.partial(spread_kernel, copies=ZL),
        out_shape=jax.ShapeDtypeStruct((ZL, count, LANES), BF16),
        in_specs=[HBM],
        out_specs=VMEM,
        scratch_shapes=[
            pltpu.VMEM(queries.shape, BF16),
            pltpu.VMEM((count, LANES), F32),
            pltpu.SemaphoreType.DMA(()),
        ],
        compiler_params=params(16),
        name="spread",
    )(pltpu.with_memory_space_constraint(queries, pltpu.HBM))


def local_kernel(
    len_ref, q_ref, cache_ref, new_ref, numer_ref, stat_ref, kv_ref, new_pad, s_ref, sems, *, heads, chunk, factor
):
    rows = q_ref.shape[1]
    group = rows // heads
    total = cache_ref.shape[0]
    news = new_ref.shape[0]
    new_pad[...] = jnp.zeros_like(new_pad)
    pieces = sems.shape[0] - 1
    size = total // pieces
    copies = [
        pltpu.make_async_copy(cache_ref.at[pl.ds(i * size, size)], kv_ref.at[pl.ds(i * size, size)], sems.at[i])
        for i in range(pieces)
    ]
    copies.append(pltpu.make_async_copy(new_ref, new_pad.at[pl.ds(0, news)], sems.at[pieces]))
    for copy in copies:
        copy.start()
    q = q_ref[0]
    lane = lax.broadcasted_iota(jnp.int32, (rows, chunk), 1)
    row = lax.broadcasted_iota(jnp.int32, (rows, chunk), 0)
    own = (lane % heads) == (row // group)
    limit = jnp.where(own, lane, total)
    used = len_ref[0] * heads
    peak = None
    for j in range(total // chunk):
        if j * chunk % size == 0:
            copies[j * chunk // size].wait()
        s = lax.dot_general(
            q, kv_ref[j * chunk : (j + 1) * chunk, :LANES], (((1,), (1,)), ((), ())), preferred_element_type=F32
        )
        s = jnp.where(limit < used - j * chunk, s, MASKED)
        s_ref[:, j * chunk : (j + 1) * chunk] = s
        for i in range(chunk // LANES):
            part = s[:, i * LANES : (i + 1) * LANES]
            peak = part if peak is None else jnp.maximum(peak, part)
    copies[pieces].wait()
    s_new = lax.dot_general(q, new_pad[:, :LANES], (((1,), (1,)), ((), ())), preferred_element_type=F32)
    steps = news // heads
    lane = lane[:, :LANES]
    row = row[:, :LANES]
    valid = own[:, :LANES] & (lane // heads <= row % steps)
    s_new = jnp.where(valid, s_new, MASKED)
    peak = jnp.max(jnp.maximum(peak, s_new), axis=1, keepdims=True)
    p_new = jnp.exp2((s_new - peak) * factor)
    weight = p_new
    numer = jnp.dot(p_new.astype(BF16), new_pad[:, LANES:], preferred_element_type=F32)
    for j in range(total // chunk):
        p = jnp.exp2((s_ref[:, j * chunk : (j + 1) * chunk] - peak) * factor)
        for i in range(chunk // LANES):
            weight = weight + p[:, i * LANES : (i + 1) * LANES]
        numer = numer + jnp.dot(
            p.astype(BF16), kv_ref[j * chunk : (j + 1) * chunk, LANES:], preferred_element_type=F32
        )
    numer_ref[...] = numer
    scale = factor / math.log2(math.e)
    stat_ref[...] = lane_select((rows, LANES), (peak * scale, jnp.sum(weight, axis=1, keepdims=True)))


def local(lengths, rows, cache, new, heads, factor):
    count = rows.shape[1]
    pieces = 8
    return pl.pallas_call(
        functools.partial(local_kernel, heads=heads, chunk=512, factor=factor),
        out_shape=(jax.ShapeDtypeStruct((count, LANES), F32), jax.ShapeDtypeStruct((count, LANES), F32)),
        in_specs=[SMEM, VMEM, HBM, HBM],
        out_specs=(VMEM, VMEM),
        scratch_shapes=[
            pltpu.VMEM(cache.shape, BF16),
            pltpu.VMEM((LANES, 2 * LANES), BF16),
            pltpu.VMEM((count, cache.shape[0]), F32),
            pltpu.SemaphoreType.DMA((pieces + 1,)),
        ],
        compiler_params=params(24),
        name="local",
    )(lengths, rows, *(pltpu.with_memory_space_constraint(a, pltpu.HBM) for a in (cache, new)))


def document_kernel(*refs, groups, fetch, tile, chunk, factor):
    q_refs, kv = refs[:groups], list(refs[groups : groups + 2])
    out_refs = refs[groups + 2 : 2 * groups + 2]
    held = refs[2 * groups + 2 : 2 * groups + 4]
    rows = q_refs[0].shape[0]
    positions = kv[0].shape[0]
    copies = []
    if fetch:
        far_ref, (kv[1], sems) = kv[1], refs[2 * groups + 4 :]
        size = positions // sems.shape[0]
        for i in range(sems.shape[0]):
            at = pl.ds(i * size, size)
            copies.append(pltpu.make_async_copy(far_ref.at[at], kv[1].at[at], sems.at[i]))
            copies[i].start()
    pieces = positions // chunk
    tiles = rows // tile
    units = [(g, b, r) for g in range(groups) for b in range(2) for r in range(tiles)]
    scale = factor / math.log2(math.e)

    def scores(u, j):
        g, b, r = units[u]
        if u == tiles and j == 0:
            for copy in copies:
                copy.wait()
        s = lax.dot_general(
            q_refs[g][r * tile : (r + 1) * tile, :],
            kv[b][j * chunk : (j + 1) * chunk, :LANES],
            (((1,), (1,)), ((), ())),
            preferred_element_type=F32,
        )
        held[u % 2][:, j * chunk : (j + 1) * chunk] = s
        peak = s[:, :LANES]
        for i in range(1, chunk // LANES):
            peak = jnp.maximum(peak, s[:, i * LANES : (i + 1) * LANES])
        return peak

    running = None
    for j in range(pieces):
        part = scores(0, j)
        running = part if running is None else jnp.maximum(running, part)
    done = {}
    stats = []
    for u, (g, b, r) in enumerate(units):
        peak = jnp.max(running, axis=1, keepdims=True)
        running = total = numer = None
        for j in range(pieces):
            if u + 1 < len(units):
                part = scores(u + 1, j)
                running = part if running is None else jnp.maximum(running, part)
            p = jnp.exp2((held[u % 2][:, j * chunk : (j + 1) * chunk] - peak) * factor)
            for i in range(chunk // LANES):
                part = p[:, i * LANES : (i + 1) * LANES]
                total = part if total is None else total + part
            part = jnp.dot(
                p.astype(BF16), kv[b][j * chunk : (j + 1) * chunk, LANES:], preferred_element_type=F32
            )
            numer = part if numer is None else numer + part
        done[b, r] = (peak, jnp.sum(total, axis=1, keepdims=True), numer)
        if b == 1:
            (peak0, total0, numer0), (peak1, total1, numer1) = done[0, r], done[1, r]
            base = toward_zero(jnp.maximum(peak0, peak1) * (2.0 * scale))
            ground = base * (0.5 / scale)
            factor0 = jnp.exp2((peak0 - ground) * factor)
            factor1 = jnp.exp2((peak1 - ground) * factor)
            coded, power = code(numer0 * factor0 + numer1 * factor1)
            out_refs[g][r * tile : (r + 1) * tile, :] = coded
            weight = total0 * factor0 + total1 * factor1
            for i in range(tile // LANES):
                at = slice(i * LANES, (i + 1) * LANES)
                stats.append((base[at], weight[at], weight[at], power[at]))
            if len(stats) * LANES == rows:
                side = lane_select((LANES, LANES), [stat[j] for j in range(4) for stat in stats])
                whole, part = split_weight(side)
                lane = lax.broadcasted_iota(jnp.int32, (LANES, LANES), 1) // len(stats)
                side = jnp.where(lane == 1, whole, jnp.where(lane == 2, part, side))
                out_refs[g][rows : rows + LANES, :] = side.astype(jnp.int32).astype(jnp.int16)
                stats = []


def document(groups, kv0, kv1, factor, fetch=False):
    count = groups[0].shape[0]
    tile = 256
    out = jax.ShapeDtypeStruct((count + LANES, LANES), jnp.int16)
    scratch = [pltpu.VMEM((tile, kv0.shape[0]), F32)] * 2
    if fetch:
        kv1 = pltpu.with_memory_space_constraint(kv1, pltpu.HBM)
        scratch += [pltpu.VMEM(kv1.shape, BF16), pltpu.SemaphoreType.DMA((2,))]
    return pl.pallas_call(
        functools.partial(
            document_kernel, groups=len(groups), fetch=fetch, tile=tile, chunk=512, factor=factor
        ),
        out_shape=[out] * len(groups),
        in_specs=[VMEM] * (len(groups) + 1) + [HBM if fetch else VMEM],
        out_specs=[VMEM] * len(groups),
        scratch_shapes=scratch,
        compiler_params=params(40),
        name="document",
    )(*groups, kv0, kv1)


def merge_kernel(*refs):
    parts, out_ref = refs[:-1], refs[-1]
    blocks = 4
    owners = LANES // 16
    rows = parts[0].shape[0] - LANES
    lane = lax.broadcasted_iota(jnp.int32, (LANES, LANES), 1)

    def shifted(values, lanes):
        return pltpu.roll(values, lanes % LANES, 1)

    stats = [p[rows : rows + LANES, :].astype(jnp.int32).astype(F32) for p in parts]
    top = functools.reduce(jnp.maximum, stats)
    shrink = [jnp.exp(jnp.minimum(s - top, 0.0) * 0.5) for s in stats]
    weight = sum(f * join_weight(shifted(s, -blocks), shifted(s, -2 * blocks)) for f, s in zip(shrink, stats))
    whole, part = split_weight(weight)
    scales = [f * jnp.exp2(shifted(s, -3 * blocks) - BITS) for f, s in zip(shrink, stats)]
    side = jnp.where(lane < blocks, top, jnp.where(lane < 2 * blocks, shifted(whole, blocks), shifted(part, 2 * blocks)))
    for b in range(blocks):
        numer = None
        for p, scale in zip(parts, scales):
            term = p[b * LANES : (b + 1) * LANES, :].astype(jnp.int32).astype(F32) * scale[:, b : b + 1]
            numer = term if numer is None else numer + term
        coded, power = code(numer)
        tile = side if b == 0 else shifted(side, -b)
        tile = jnp.where(lane < 3 * blocks, tile, power).astype(jnp.int32).astype(jnp.int16)
        for s in range(owners):
            out_ref[b * owners + s, 0:16, :] = coded[16 * s : 16 * (s + 1), :]
            out_ref[b * owners + s, 16:32, :] = tile[16 * s : 16 * (s + 1), :]


def merge(parts):
    return pl.pallas_call(
        merge_kernel,
        out_shape=jax.ShapeDtypeStruct((32, 32, LANES), jnp.int16),
        in_specs=[VMEM] * len(parts),
        out_specs=VMEM,
        compiler_params=params(32),
        name="merge",
    )(*parts)


def finish_kernel(got_ref, numer_ref, stat_ref, out_ref, rows_ref, *, heads):
    steps = out_ref.shape[1]
    rows = numer_ref.shape[0]

    def read(z, first):
        part = got_ref[z * heads : (z + 1) * heads, first : first + 16, :]
        return part.astype(jnp.int32).astype(F32).reshape(rows, LANES)

    tiles = [read(z, 16) for z in range(ZL)]
    peak = stat_ref[:, 0:1]
    tops = [t[:, 0:1] * 0.5 for t in tiles]
    top = functools.reduce(jnp.maximum, tops, peak)
    shrink = jnp.exp(peak - top)
    numer = numer_ref[...] * shrink
    weight = stat_ref[:, 1:2] * shrink
    for z, t in enumerate(tiles):
        shrink = jnp.exp(tops[z] - top)
        weight = weight + shrink * join_weight(t[:, 4:5], t[:, 8:9])
        numer = numer + read(z, 0) * (shrink * jnp.exp2(t[:, 12:13] - BITS))
    rows_ref[...] = numer / weight
    for c in range(out_ref.shape[2] // LANES):
        out_ref[0, :, LANES * c : LANES * (c + 1)] = rows_ref[steps * c : steps * (c + 1), :].astype(BF16)


def finish(got, numer, stat, shape, heads):
    return pl.pallas_call(
        functools.partial(finish_kernel, heads=heads),
        out_shape=jax.ShapeDtypeStruct(shape, BF16),
        in_specs=[VMEM] * 3,
        out_specs=VMEM,
        scratch_shapes=[pltpu.VMEM(numer.shape, F32)],
        compiler_params=params(16),
        name="finish",
    )(got, numer, stat)


def per_device(queries, prefix_kv, suffix_kv, new_kv, lengths):
    positions, _, width = prefix_kv.shape
    head_dim = width // 2
    heads = suffix_kv.shape[2]
    factor = math.log2(math.e) / math.sqrt(head_dim)
    kv_own = prefix_kv.reshape(positions, width)
    kv_other = lax.ppermute(kv_own, "core", [(0, 1), (1, 0)])
    spread_rows = spread(queries)
    gathered = lax.all_to_all(
        spread_rows.reshape(ZL * heads, 16, LANES), WIDE, split_axis=0, concat_axis=0, tiled=True
    ).reshape(-1, LANES)
    others = [lax.ppermute(gathered, "y", [(j, (j - d) % Y) for j in range(Y)]) for d in (1, 3, 2)]
    parts = document(others[:1], kv_other, kv_own, factor, fetch=True)
    parts, others = lax.optimization_barrier((parts, others))
    parts += document(others[1:], kv_own, kv_other, factor)
    parts = [lax.ppermute(p, "y", [(j, (j + d) % Y) for j in range(Y)]) for d, p in zip((1, 3, 2), parts)]
    parts += document([gathered], kv_own, kv_other, factor)
    merged = merge(parts)
    merged, spread_rows = lax.optimization_barrier((merged, spread_rows))
    got = lax.all_to_all(merged, WIDE, split_axis=0, concat_axis=0, tiled=True)
    cache = suffix_kv.reshape(-1, width)
    numer, stat = local(lengths, spread_rows, cache, new_kv.reshape(-1, width), heads, factor)
    return finish(got, numer, stat, queries.shape, heads)


def solution(mesh):
    devices = mesh.devices.reshape(Y, ZL, CORE, X, ZH)
    fine = Mesh(devices, AXES)
    prefix, sample = ("y", "zl", "core"), ("x", "zh")
    owner = P(prefix + sample)
    in_specs = (owner, P(prefix, sample), owner, owner, owner)
    return jax.shard_map(per_device, mesh=fine, in_specs=in_specs, out_specs=owner, check_vma=False)
```

time: 81.6 us -> 76.5 us (0.938)
  local copies, waits for them, and re-layouts: 4.54 us -> 0.01 us
    unnamed x10 -> x2, local copies, waits for them, and re-layouts: 4.54 us -> 0.01 us
    pallas_call x1, Pallas kernels: 3.96 us -> 1.73 us  [finish(): pl.pallas_call(functools.partial(finish_kernel, heads=heads), out_shape=j...]
    pallas_call x1, Pallas kernels: 2.22 us -> 4.44 us  [local(): pl.pallas_call(functools.partial(local_kernel, heads=heads, chunk=512, fa...]
    pallas_call x4 -> x3, Pallas kernels: 23.5 us -> 22.4 us  [document(): pl.pallas_call(functools.partial(document_kernel, groups=len(groups), fet...]
  transfers between devices with their start and end apart: 8 -> 8, of which waited for: 2 -> 2; matrix products, arithmetic and copies ran while one was open for 0% -> 0% of each run, Pallas kernels for 32% -> 36%
where the time goes in v2:
time: 76.5 us; the launch traced here: 76.3 us
  Pallas kernels  31 us (41%)
  blocking collectives  21.5 us (28%)
  starting transfers between devices  16.5 us (22%)
  waiting for transfers between devices  6.53 us (9%)
    pallas_call x3, Pallas kernels, document(): pl.pallas_call(functools.partial(document_kernel, groups=len(groups), fet...  22.4 us
    all_to_all x1, blocking collectives, per_device(): lax.all_to_all(spread_rows.reshape(ZL * heads, 16, LANES), WIDE, split_ax...  21.5 us
    ppermute x3, starting transfers between devices, per_device(): lax.ppermute(p, 'y', [(j, (j + d) % Y) for j in range(Y)])  7.12 us
    all_to_all x1, waiting for transfers between devices, per_device(): got = lax.all_to_all(merged, WIDE, split_axis=0, concat_axis=0, tiled=True)  6.14 us
    ppermute x3, starting transfers between devices, per_device(): lax.ppermute(gathered, 'y', [(j, (j - d) % Y) for j in range(Y)])  5.22 us
    pallas_call x1, Pallas kernels, local(): pl.pallas_call(functools.partial(local_kernel, heads=heads, chunk=512, fa...  4.44 us
    all_to_all x1, starting transfers between devices, per_device(): got = lax.all_to_all(merged, WIDE, split_axis=0, concat_axis=0, tiled=True)  4.14 us
    pallas_call x1, Pallas kernels, finish(): pl.pallas_call(functools.partial(finish_kernel, heads=heads), out_shape=j...  1.73 us
  transfers between devices with their start and end apart: 8, of which 2 were waited for; matrix products, arithmetic and copies ran while one was open for 0% of the time, Pallas kernels for 36%

profile of v2, /device:TPU:32, one launch (start us, length us, event | category | flops | bytes accessed | tf_op | source)
XLA Modules:
  0.0 76.3 jit_solution(3603662805024031470)
XLA Ops:
  0.0 0.0 collective-permute-start.1
  0.0 0.8 %spread.1.q_ref = bf16[4,128,128]{2,1,0:T(8,128)(2,1)S(1)} custom-call(bf16[1,2,8192]{2,1,0:T(2,128)(2,1)} %q_ref.1), custom_call_target="tpu_custom_call" | custom-call | tf_op jit(solution)/shard_map/spread/pallas_call | solution.py:72
  0.8 21.5 %all_to_all.10 = bf16[32,16,128]{2,1,0:T(8,128)(2,1)S(1)} all-to-all(bf16[32,16,128]{2,1,0:T(8,128)(2,1)S(1)} %bitcast.9), channel_id=1, replica_groups=mesh['y'=4,'zl'=4,'core'=2,'x'=4,'zh'=2] {'zl','x','zh'}, dimensions={0} | all-to-all | bytes 262144 | tf_op jit(solution)/shard_map/all_to_all | solution.py:349
  22.3 0.0 copy-start
  22.3 3.0 %collective-permute-start = (bf16[512,128]{1,0:T(8,128)(2,1)S(1)}, bf16[512,128]{1,0:T(8,128)(2,1)S(1)}, u32[]{:S(2)}, u32[]{:S(2)}) collective-permute-start(bf16[512,128]{1,0:T(8,128)(2,1)S(1)} %bitcast.10), channel_id=1, source_target_pairs={{0,192},{64,0},{128,64},{192,128},{1,193},{65,1},{129,65},{193,129... | collective-permute-start | bytes 393224 | tf_op jit(solution)/shard_map/ppermute | solution.py:352
  25.3 0.0 collective-permute-start.2
  25.4 2.2 %collective-permute-start.3 = (bf16[512,128]{1,0:T(8,128)(2,1)S(1)}, bf16[512,128]{1,0:T(8,128)(2,1)S(1)}, u32[]{:S(2)}, u32[]{:S(2)}) collective-permute-start(bf16[512,128]{1,0:T(8,128)(2,1)S(1)} %bitcast.12), channel_id=1, source_target_pairs={{0,128},{64,192},{128,0},{192,64},{1,129},{65,193},{129,1},{193,65... | collective-permute-start | bytes 393224 | tf_op jit(solution)/shard_map/ppermute | solution.py:352
  27.6 0.4 collective-permute-done.refs_0_
  27.9 0.0 collective-permute-done.1.refs_1_.refs_3_.refs_2_
  27.9 6.2 %document.3 = s16[640,128]{1,0:T(8,128)(2,1)S(1)} custom-call(bf16[512,128]{1,0:T(8,128)(2,1)S(1)} %collective-permute-done.refs_0_, bf16[4096,256]{1,0:T(8,128)(2,1)S(1)} %collective-permute-done.1.refs_1_.refs_3_.refs_2_, bf16[4096,256]{1,0:T(8,128)(2,1)} %bitcast.6), custom_call_target="tpu_custom_call" | custom-call | tf_op jit(solution)/shard_map/document/pallas_call | solution.py:251
  34.2 0.0 collective-permute-done.2.refs_0_
  34.2 0.0 collective-permute-done.3.refs_1_
  34.2 1.8 %collective-permute-start.4 = (s16[640,128]{1,0:T(8,128)(2,1)S(1)}, s16[640,128]{1,0:T(8,128)(2,1)S(1)}, u32[]{:S(2)}, u32[]{:S(2)}) collective-permute-start(s16[640,128]{1,0:T(8,128)(2,1)S(1)} %document.3), channel_id=1, source_target_pairs={{0,64},{64,128},{128,192},{192,0},{1,65},{65,129},{129,193},{193,1... | collective-permute-start | bytes 491528 | tf_op jit(solution)/shard_map/ppermute | solution.py:356
  36.0 0.0 copy-done
  36.0 10.6 %document.4 = (s16[640,128]{1,0:T(8,128)(2,1)S(1)}, s16[640,128]{1,0:T(8,128)(2,1)S(1)}) custom-call(bf16[512,128]{1,0:T(8,128)(2,1)S(1)} %collective-permute-done.2.refs_0_, bf16[512,128]{1,0:T(8,128)(2,1)S(1)} %collective-permute-done.3.refs_1_, bf16[4096,256]{1,0:T(8,128)(2,1)S(1)} %bitcast.7, ...), custom_call_target="tpu_custom_call" | custom-call | tf_op jit(solution)/shard_map/document/pallas_call | solution.py:251
  46.6 3.6 %collective-permute-start.5 = (s16[640,128]{1,0:T(8,128)(2,1)S(1)}, s16[640,128]{1,0:T(8,128)(2,1)S(1)}, u32[]{:S(2)}, u32[]{:S(2)}) collective-permute-start(s16[640,128]{1,0:T(8,128)(2,1)S(1)} %get-tuple-element.17), channel_id=1, source_target_pairs={{0,192},{64,0},{128,64},{192,128},{1,193},{65,1},{129,65},{193,129... | collective-permute-start | bytes 491528 | tf_op jit(solution)/shard_map/ppermute | solution.py:356
  50.1 1.8 %collective-permute-start.6 = (s16[640,128]{1,0:T(8,128)(2,1)S(1)}, s16[640,128]{1,0:T(8,128)(2,1)S(1)}, u32[]{:S(2)}, u32[]{:S(2)}) collective-permute-start(s16[640,128]{1,0:T(8,128)(2,1)S(1)} %get-tuple-element.18), channel_id=1, source_target_pairs={{0,128},{64,192},{128,0},{192,64},{1,129},{65,193},{129,1},{193,65... | collective-permute-start | bytes 491528 | tf_op jit(solution)/shard_map/ppermute | solution.py:356
  51.9 5.5 %document.5.refs_3_ = s16[640,128]{1,0:T(8,128)(2,1)S(1)} custom-call(bf16[512,128]{1,0:T(8,128)(2,1)S(1)} %bitcast.13, bf16[4096,256]{1,0:T(8,128)(2,1)S(1)} %bitcast.8, bf16[4096,256]{1,0:T(8,128)(2,1)S(1)} %collective-permute-done.1.refs_1_.refs_3_.refs_2_), custom_call_target="tpu_custom_call" | custom-call | tf_op jit(solution)/shard_map/document/pallas_call | solution.py:251
  57.5 0.0 collective-permute-done.4.refs_0_
  57.5 0.0 collective-permute-done.5.refs_1_
  57.5 0.0 collective-permute-done.6.refs_2_
  57.5 1.7 %merge.1 = s16[32,32,128]{2,1,0:T(8,128)(2,1)} custom-call(s16[640,128]{1,0:T(8,128)(2,1)S(1)} %collective-permute-done.4.refs_0_, s16[640,128]{1,0:T(8,128)(2,1)S(1)} %collective-permute-done.5.refs_1_, s16[640,128]{1,0:T(8,128)(2,1)S(1)} %collective-permute-done.6.refs_2_, s16[640,128]{1,0:T(8,128)(2,1)S(1)} %document.5.refs_3_), custom_call_target="tpu_custom_call" | custom-call | tf_op jit(solution)/shard_map/merge/pallas_call | solution.py:295
  59.2 4.1 %all-to-all-start.1 = ((s16[32,32,128]{2,1,0:T(8,128)(2,1)}), s16[32,32,128]{2,1,0:T(8,128)(2,1)S(1)}, u32[]{:S(2)}, u32[]{:S(2)}) async-start(s16[32,32,128]{2,1,0:T(8,128)(2,1)} %merge.1), calls=%async_computation.1 | async-start | bytes 524288 | tf_op jit(solution)/shard_map/all_to_all | solution.py:360
  64.0 4.4 %local.1 = (f32[128,128]{1,0:T(8,128)S(1)}, f32[128,128]{1,0:T(8,128)S(1)}) custom-call(s32[1]{0:T(128)S(6)} %copy.6.len_ref, bf16[4,128,128]{2,1,0:T(8,128)(2,1)S(1)} %spread.1.q_ref, bf16[8192,256]{1,0:T(8,128)(2,1)} %bitcast.14, bf16[16,256]{1,0:T(8,128)(2,1)} %bitcast.15), custom_call_target="tpu_custom_call" | custom-call | tf_op jit(solution)/shard_map/local/pallas_call | solution.py:148
  68.4 6.1 %all-to-all-done.1.got_ref = s16[32,32,128]{2,1,0:T(8,128)(2,1)S(1)} async-done(((s16[32,32,128]{2,1,0:T(8,128)(2,1)}), s16[32,32,128]{2,1,0:T(8,128)(2,1)S(1)}, u32[]{:S(2)}, u32[]{:S(2)}) %all-to-all-start.1) | async-done | bytes 262176 | tf_op jit(solution)/shard_map/all_to_all | solution.py:360
  74.5 1.7 %finish.1 = bf16[1,2,8192]{2,1,0:T(2,128)(2,1)} custom-call(s16[32,32,128]{2,1,0:T(8,128)(2,1)S(1)} %all-to-all-done.1.got_ref, f32[128,128]{1,0:T(8,128)S(1)} %get-tuple-element.21.numer_ref, f32[128,128]{1,0:T(8,128)S(1)} %get-tuple-element.22.stat_ref), custom_call_target="tpu_custom_call" | custom-call | tf_op jit(solution)/shard_map/finish/pallas_call | solution.py:330
Async XLA Ops:
  0.0 27.9 %collective-permute-start.1 = (bf16[4096,256]{1,0:T(8,128)(2,1)}, bf16[4096,256]{1,0:T(8,128)(2,1)S(1)}, u32[]{:S(2)}, u32[]{:S(2)}) collective-permute-start(bf16[4096,256]{1,0:T(8,128)(2,1)} %bitcast.5), channel_id=1, source_target_pairs={{0,8},{8,0},{1,9},{9,1},{2,10},{10,2},{3,11},{11,3},{4,12},{12,4},... | collective-permute-start | bytes 6291464 | tf_op jit(solution)/shard_map/ppermute | solution.py:347
  22.3 13.7 %copy-start = (bf16[4096,1,256]{2,0,1:T(8,128)(2,1)S(1)}, bf16[4096,1,256]{2,0,1:T(8,128)(2,1)}, u32[]{:S(2)}) copy-start(bf16[4096,1,256]{2,0,1:T(8,128)(2,1)} %param.6) | copy-start | bytes 6291460
  22.3 5.6 %collective-permute-start = (bf16[512,128]{1,0:T(8,128)(2,1)S(1)}, bf16[512,128]{1,0:T(8,128)(2,1)S(1)}, u32[]{:S(2)}, u32[]{:S(2)}) collective-permute-start(bf16[512,128]{1,0:T(8,128)(2,1)S(1)} %bitcast.10), channel_id=1, source_target_pairs={{0,192},{64,0},{128,64},{192,128},{1,193},{65,1},{129,65},{193,129... | collective-permute-start | bytes 393224 | tf_op jit(solution)/shard_map/ppermute | solution.py:352
  25.3 8.8 %collective-permute-start.2 = (bf16[512,128]{1,0:T(8,128)(2,1)S(1)}, bf16[512,128]{1,0:T(8,128)(2,1)S(1)}, u32[]{:S(2)}, u32[]{:S(2)}) collective-permute-start(bf16[512,128]{1,0:T(8,128)(2,1)S(1)} %bitcast.11), channel_id=1, source_target_pairs={{0,64},{64,128},{128,192},{192,0},{1,65},{65,129},{129,193},{193,1... | collective-permute-start | bytes 393224 | tf_op jit(solution)/shard_map/ppermute | solution.py:352
  25.4 8.8 %collective-permute-start.3 = (bf16[512,128]{1,0:T(8,128)(2,1)S(1)}, bf16[512,128]{1,0:T(8,128)(2,1)S(1)}, u32[]{:S(2)}, u32[]{:S(2)}) collective-permute-start(bf16[512,128]{1,0:T(8,128)(2,1)S(1)} %bitcast.12), channel_id=1, source_target_pairs={{0,128},{64,192},{128,0},{192,64},{1,129},{65,193},{129,1},{193,65... | collective-permute-start | bytes 393224 | tf_op jit(solution)/shard_map/ppermute | solution.py:352
  34.2 23.3 %collective-permute-start.4 = (s16[640,128]{1,0:T(8,128)(2,1)S(1)}, s16[640,128]{1,0:T(8,128)(2,1)S(1)}, u32[]{:S(2)}, u32[]{:S(2)}) collective-permute-start(s16[640,128]{1,0:T(8,128)(2,1)S(1)} %document.3), channel_id=1, source_target_pairs={{0,64},{64,128},{128,192},{192,0},{1,65},{65,129},{129,193},{193,1... | collective-permute-start | bytes 491528 | tf_op jit(solution)/shard_map/ppermute | solution.py:356
  46.6 10.9 %collective-permute-start.5 = (s16[640,128]{1,0:T(8,128)(2,1)S(1)}, s16[640,128]{1,0:T(8,128)(2,1)S(1)}, u32[]{:S(2)}, u32[]{:S(2)}) collective-permute-start(s16[640,128]{1,0:T(8,128)(2,1)S(1)} %get-tuple-element.17), channel_id=1, source_target_pairs={{0,192},{64,0},{128,64},{192,128},{1,193},{65,1},{129,65},{193,129... | collective-permute-start | bytes 491528 | tf_op jit(solution)/shard_map/ppermute | solution.py:356
  50.1 7.3 %collective-permute-start.6 = (s16[640,128]{1,0:T(8,128)(2,1)S(1)}, s16[640,128]{1,0:T(8,128)(2,1)S(1)}, u32[]{:S(2)}, u32[]{:S(2)}) collective-permute-start(s16[640,128]{1,0:T(8,128)(2,1)S(1)} %get-tuple-element.18), channel_id=1, source_target_pairs={{0,128},{64,192},{128,0},{192,64},{1,129},{65,193},{129,1},{193,65... | collective-permute-start | bytes 491528 | tf_op jit(solution)/shard_map/ppermute | solution.py:356
  59.2 15.4 %all-to-all-start.1 = ((s16[32,32,128]{2,1,0:T(8,128)(2,1)}), s16[32,32,128]{2,1,0:T(8,128)(2,1)S(1)}, u32[]{:S(2)}, u32[]{:S(2)}) async-start(s16[32,32,128]{2,1,0:T(8,128)(2,1)} %merge.1), calls=%async_computation.1 | async-start | bytes 524288 | tf_op jit(solution)/shard_map/all_to_all | solution.py:360

commit v3 on v2

--- a/solution.py
+++ b/solution.py
@@ -11,9 +11,10 @@
 F32 = jnp.float32
 BF16 = jnp.bfloat16
 LANES = 128
-Y, ZL, CORE, X, ZH = 4, 4, 2, 4, 2
-AXES = ("y", "zl", "core", "x", "zh")
+YH, YL, ZL, CORE, X, ZH = 2, 2, 4, 2, 4, 2
+AXES = ("yh", "yl", "zl", "core", "x", "zh")
 WIDE = ("zl", "x", "zh")
+SWAP = [(0, 1), (1, 0)]
 BITS = 14.9
 FRACTION = 32767.0
 MASKED = -1e30
@@ -70,8 +71,8 @@
 def spread(queries):
     count = queries.shape[1] * queries.shape[2] // LANES
     return pl.pallas_call(
-        functools.partial(spread_kernel, copies=ZL),
-        out_shape=jax.ShapeDtypeStruct((ZL, count, LANES), BF16),
+        functools.partial(spread_kernel, copies=YL * ZL),
+        out_shape=jax.ShapeDtypeStruct((YL * ZL, count, LANES), BF16),
         in_specs=[HBM],
         out_specs=VMEM,
         scratch_shapes=[
@@ -161,15 +162,18 @@
     )(lengths, rows, *(pltpu.with_memory_space_constraint(a, pltpu.HBM) for a in (cache, new)))
 
 
-def document_kernel(*refs, groups, fetch, tile, chunk, factor):
-    q_refs, kv = refs[:groups], list(refs[groups : groups + 2])
-    out_refs = refs[groups + 2 : 2 * groups + 2]
-    held = refs[2 * groups + 2 : 2 * groups + 4]
-    rows = q_refs[0].shape[0]
+def document_kernel(low_ref, q_ref, *refs, picks, fetch, tile, chunk, factor):
+    groups = len(picks)
+    kv = list(refs[:2])
+    out_refs = refs[2 : groups + 2]
+    held = refs[groups + 2 : groups + 4]
+    rows = q_ref.shape[1]
+    low = low_ref[0]
+    blocks_of = [1 - low if pick else low for pick in picks]
     positions = kv[0].shape[0]
     copies = []
     if fetch:
-        far_ref, (kv[1], sems) = kv[1], refs[2 * groups + 4 :]
+        far_ref, (kv[1], sems) = kv[1], refs[groups + 4 :]
         size = positions // sems.shape[0]
         for i in range(sems.shape[0]):
             at = pl.ds(i * size, size)
@@ -186,7 +190,7 @@
             for copy in copies:
                 copy.wait()
         s = lax.dot_general(
-            q_refs[g][r * tile : (r + 1) * tile, :],
+            q_ref[blocks_of[g], r * tile : (r + 1) * tile, :],
             kv[b][j * chunk : (j + 1) * chunk, :LANES],
             (((1,), (1,)), ((), ())),
             preferred_element_type=F32,
@@ -240,25 +244,22 @@
                 stats = []
 
 
-def document(groups, kv0, kv1, factor, fetch=False):
-    count = groups[0].shape[0]
+def document(low, pair, picks, kv0, kv1, factor, fetch=False):
     tile = 256
-    out = jax.ShapeDtypeStruct((count + LANES, LANES), jnp.int16)
+    out = jax.ShapeDtypeStruct((pair.shape[1] + LANES, LANES), jnp.int16)
     scratch = [pltpu.VMEM((tile, kv0.shape[0]), F32)] * 2
     if fetch:
         kv1 = pltpu.with_memory_space_constraint(kv1, pltpu.HBM)
         scratch += [pltpu.VMEM(kv1.shape, BF16), pltpu.SemaphoreType.DMA((2,))]
     return pl.pallas_call(
-        functools.partial(
-            document_kernel, groups=len(groups), fetch=fetch, tile=tile, chunk=512, factor=factor
-        ),
-        out_shape=[out] * len(groups),
-        in_specs=[VMEM] * (len(groups) + 1) + [HBM if fetch else VMEM],
-        out_specs=[VMEM] * len(groups),
+        functools.partial(document_kernel, picks=picks, fetch=fetch, tile=tile, chunk=512, factor=factor),
+        out_shape=[out] * len(picks),
+        in_specs=[SMEM, VMEM, VMEM, HBM if fetch else VMEM],
+        out_specs=[VMEM] * len(picks),
         scratch_shapes=scratch,
         compiler_params=params(40),
         name="document",
-    )(*groups, kv0, kv1)
+    )(low, pair, kv0, kv1)
 
 
 def merge_kernel(*refs):
@@ -344,17 +345,34 @@
     heads = suffix_kv.shape[2]
     factor = math.log2(math.e) / math.sqrt(head_dim)
     kv_own = prefix_kv.reshape(positions, width)
-    kv_other = lax.ppermute(kv_own, "core", [(0, 1), (1, 0)])
+    kv_other = lax.ppermute(kv_own, "core", SWAP)
+    low = lax.axis_index("yl").astype(jnp.int32).reshape(1)
+
+    def after(array, *earlier):
+        return lax.optimization_barrier((array, earlier))[0]
+
+    def across(array):
+        return lax.ppermute(array, "yh", SWAP)
+
+    def diagonal(array):
+        return lax.ppermute(array, ("yh", "yl"), [(j, YH * YL - 1 - j) for j in range(YH * YL)])
+
     spread_rows = spread(queries)
-    gathered = lax.all_to_all(
-        spread_rows.reshape(ZL * heads, 16, LANES), WIDE, split_axis=0, concat_axis=0, tiled=True
-    ).reshape(-1, LANES)
-    others = [lax.ppermute(gathered, "y", [(j, (j - d) % Y) for j in range(Y)]) for d in (1, 3, 2)]
-    parts = document(others[:1], kv_other, kv_own, factor, fetch=True)
-    parts, others = lax.optimization_barrier((parts, others))
-    parts += document(others[1:], kv_own, kv_other, factor)
-    parts = [lax.ppermute(p, "y", [(j, (j + d) % Y) for j in range(Y)]) for d, p in zip((1, 3, 2), parts)]
-    parts += document([gathered], kv_own, kv_other, factor)
+    count = spread_rows.shape[0] * heads
+    pair = lax.all_to_all(
+        spread_rows.reshape(count, -1, LANES), ("yl",) + WIDE, split_axis=0, concat_axis=0, tiled=True
+    ).reshape(YL, -1, LANES)
+    far = diagonal(pair)
+    near_part = document(low, pair, (1,), kv_other, kv_own, factor, fetch=True)
+    near_part, far = lax.optimization_barrier((near_part, far))
+    far_parts = document(low, far, (1, 0), kv_own, kv_other, factor)
+    own_part = document(low, after(pair, far_parts), (0,), kv_own, kv_other, factor)
+    parts = [
+        own_part[0],
+        lax.ppermute(near_part[0], "yl", SWAP),
+        diagonal(far_parts[0]),
+        across(far_parts[1]),
+    ]
     merged = merge(parts)
     merged, spread_rows = lax.optimization_barrier((merged, spread_rows))
     got = lax.all_to_all(merged, WIDE, split_axis=0, concat_axis=0, tiled=True)
@@ -364,9 +382,9 @@
 
 
 def solution(mesh):
-    devices = mesh.devices.reshape(Y, ZL, CORE, X, ZH)
+    devices = mesh.devices.reshape(YH, YL, ZL, CORE, X, ZH)
     fine = Mesh(devices, AXES)
-    prefix, sample = ("y", "zl", "core"), ("x", "zh")
+    prefix, sample = AXES[:4], AXES[4:]
     owner = P(prefix + sample)
     in_specs = (owner, P(prefix, sample), owner, owner, owner)
     return jax.shard_map(per_device, mesh=fine, in_specs=in_specs, out_specs=owner, check_vma=False)

time: 76.5 us -> 76.5 us (level)
  starting transfers between devices: 16.5 us -> 11.4 us
  blocking collectives: 21.5 us -> 25.6 us
    ppermute x7 -> x5, starting transfers between devices: 12.3 us -> 6.9 us  [the longest x2 5.33 us: diagonal(): lax.ppermute(array, ('yh', 'yl'), [(j, YH * YL - 1 - j) for j in range(YH...]
    all_to_all x1, blocking collectives: 21.5 us -> 25.6 us  [per_device(): lax.all_to_all(spread_rows.reshape(count, -1, LANES), ('yl',) + WIDE, spl...]
  transfers between devices with their start and end apart: 8 -> 6, of which waited for: 2 -> 3; matrix products, arithmetic and copies ran while one was open for 0% -> 0% of each run, Pallas kernels for 36% -> 22%
where the time goes in v3:
time: 76.5 us; the launch traced here: 76.2 us
  Pallas kernels  31.5 us (41%)
  blocking collectives  25.6 us (33%)
  starting transfers between devices  11.4 us (15%)
  waiting for transfers between devices  6.95 us (9%)
    all_to_all x1, blocking collectives, per_device(): lax.all_to_all(spread_rows.reshape(count, -1, LANES), ('yl',) + WIDE, spl...  25.6 us
    pallas_call x3, Pallas kernels, document(): pl.pallas_call(functools.partial(document_kernel, picks=picks, fetch=fetc...  22.9 us
    all_to_all x1, waiting for transfers between devices, per_device(): got = lax.all_to_all(merged, WIDE, split_axis=0, concat_axis=0, tiled=True)  6.14 us
    ppermute x2, starting transfers between devices, diagonal(): lax.ppermute(array, ('yh', 'yl'), [(j, YH * YL - 1 - j) for j in range(YH...  5.33 us
    all_to_all x1, starting transfers between devices, per_device(): got = lax.all_to_all(merged, WIDE, split_axis=0, concat_axis=0, tiled=True)  4.52 us
    pallas_call x1, Pallas kernels, local(): pl.pallas_call(functools.partial(local_kernel, heads=heads, chunk=512, fa...  4.44 us
    pallas_call x1, Pallas kernels, finish(): pl.pallas_call(functools.partial(finish_kernel, heads=heads), out_shape=j...  1.73 us
    pallas_call x1, Pallas kernels, merge(): pl.pallas_call(merge_kernel, out_shape=jax.ShapeDtypeStruct((32, 32, LANE...  1.67 us
  transfers between devices with their start and end apart: 6, of which 3 were waited for; matrix products, arithmetic and copies ran while one was open for 0% of the time, Pallas kernels for 22%

profile of v3, /device:TPU:32, one launch (start us, length us, event | category | flops | bytes accessed | tf_op | source)
XLA Modules:
  0.0 76.2 jit_solution(8364208415405460243)
XLA Ops:
  0.0 0.0 collective-permute-start
  0.0 0.8 %spread.1.q_ref = bf16[8,128,128]{2,1,0:T(8,128)(2,1)S(1)} custom-call(bf16[1,2,8192]{2,1,0:T(2,128)(2,1)} %q_ref.1), custom_call_target="tpu_custom_call" | custom-call | tf_op jit(solution)/shard_map/spread/pallas_call | solution.py:73
  0.8 25.6 %all_to_all.10 = bf16[64,16,128]{2,1,0:T(8,128)(2,1)S(1)} all-to-all(bf16[64,16,128]{2,1,0:T(8,128)(2,1)S(1)} %bitcast.13), channel_id=1, replica_groups=mesh['yh'=2,'yl'=2,'zl'=4,'core'=2,'x'=4,'zh'=2] {'yl','zl','x','zh'}, dimensions={0} | all-to-all | bytes 524288 | tf_op jit(solution)/shard_map/all_to_all | solution.py:362
  26.4 2.7 %collective-permute-start.1 = (bf16[2,512,128]{2,1,0:T(8,128)(2,1)S(1)}, bf16[2,512,128]{2,1,0:T(8,128)(2,1)S(1)}, u32[]{:S(2)}, u32[]{:S(2)}) collective-permute-start(bf16[2,512,128]{2,1,0:T(8,128)(2,1)S(1)} %bitcast.10), channel_id=1, source_target_pairs={{0,192},{64,128},{128,64},{192,0},{1,193},{65,129},{129,65},{193,1... | collective-permute-start | bytes 786440 | tf_op jit(solution)/shard_map/ppermute | solution.py:358
  29.2 0.0 collective-permute-done.refs_0_.refs_1_
  29.2 0.0 copy-start
  29.2 6.2 %document.3 = s16[640,128]{1,0:T(8,128)(2,1)S(1)} custom-call(s32[1]{0:T(128)} %bitcast.low_ref, bf16[2,512,128]{2,1,0:T(8,128)(2,1)S(1)} %bitcast.11, bf16[4096,256]{1,0:T(8,128)(2,1)S(1)} %collective-permute-done.refs_0_.refs_1_, bf16[4096,256]{1,0:T(8,128)(2,1)} %bitcast.7), custom_call_target="tpu_custom_call" | custom-call | tf_op jit(solution)/shard_map/document/pallas_call | solution.py:254
  35.4 0.0 collective-permute-done.1.q_ref
  35.4 0.0 copy-done
  35.4 11.0 %document.4 = (s16[640,128]{1,0:T(8,128)(2,1)S(1)}, s16[640,128]{1,0:T(8,128)(2,1)S(1)}) custom-call(s32[1]{0:T(128)} %bitcast.low_ref, bf16[2,512,128]{2,1,0:T(8,128)(2,1)S(1)} %collective-permute-done.1.q_ref, bf16[4096,256]{1,0:T(8,128)(2,1)S(1)} %bitcast.8, bf16[4096,256]{1,0:T(8,128)(2,1)S(1)} %collective-permute-done.refs_0_.refs_1_), custom_call_target="tpu_custom_call" | custom-call | tf_op jit(solution)/shard_map/document/pallas_call | solution.py:254
  46.4 2.6 %collective-permute-start.3 = (s16[640,128]{1,0:T(8,128)(2,1)S(1)}, s16[640,128]{1,0:T(8,128)(2,1)S(1)}, u32[]{:S(2)}, u32[]{:S(2)}) collective-permute-start(s16[640,128]{1,0:T(8,128)(2,1)S(1)} %get-tuple-element.15), channel_id=1, source_target_pairs={{0,192},{64,128},{128,64},{192,0},{1,193},{65,129},{129,65},{193,1... | collective-permute-start | bytes 491528 | tf_op jit(solution)/shard_map/ppermute | solution.py:358
  49.0 0.0 collective-permute-start.4
  49.0 1.6 %collective-permute-start.2 = (s16[640,128]{1,0:T(8,128)(2,1)S(1)}, s16[640,128]{1,0:T(8,128)(2,1)S(1)}, u32[]{:S(2)}, u32[]{:S(2)}) collective-permute-start(s16[640,128]{1,0:T(8,128)(2,1)S(1)} %document.3), channel_id=1, source_target_pairs={{0,64},{64,0},{1,65},{65,1},{2,66},{66,2},{3,67},{67,3},{4,68},{68... | collective-permute-start | bytes 491528 | tf_op jit(solution)/shard_map/ppermute | solution.py:372
  50.6 5.6 %document.5.refs_0_ = s16[640,128]{1,0:T(8,128)(2,1)S(1)} custom-call(s32[1]{0:T(128)} %bitcast.low_ref, bf16[2,512,128]{2,1,0:T(8,128)(2,1)S(1)} %bitcast.12, bf16[4096,256]{1,0:T(8,128)(2,1)S(1)} %bitcast.9, bf16[4096,256]{1,0:T(8,128)(2,1)S(1)} %collective-permute-done.refs_0_.refs_1_), custom_call_target="tpu_custom_call" | custom-call | tf_op jit(solution)/shard_map/document/pallas_call | solution.py:254
  56.2 0.0 collective-permute-done.3.refs_2_
  56.3 0.4 collective-permute-done.4.refs_3_
  56.6 0.4 collective-permute-done.2.refs_1_
  57.1 1.7 %merge.1 = s16[32,32,128]{2,1,0:T(8,128)(2,1)} custom-call(s16[640,128]{1,0:T(8,128)(2,1)S(1)} %document.5.refs_0_, s16[640,128]{1,0:T(8,128)(2,1)S(1)} %collective-permute-done.2.refs_1_, s16[640,128]{1,0:T(8,128)(2,1)S(1)} %collective-permute-done.3.refs_2_, s16[640,128]{1,0:T(8,128)(2,1)S(1)} %collective-permute-done.4.refs_3_), custom_call_target="tpu_custom_call" | custom-call | tf_op jit(solution)/shard_map/merge/pallas_call | solution.py:296
  58.7 4.5 %all-to-all-start.1 = ((s16[32,32,128]{2,1,0:T(8,128)(2,1)}), s16[32,32,128]{2,1,0:T(8,128)(2,1)S(1)}, u32[]{:S(2)}, u32[]{:S(2)}) async-start(s16[32,32,128]{2,1,0:T(8,128)(2,1)} %merge.1), calls=%async_computation.1 | async-start | bytes 524288 | tf_op jit(solution)/shard_map/all_to_all | solution.py:378
  63.9 4.4 %local.1 = (f32[128,128]{1,0:T(8,128)S(1)}, f32[128,128]{1,0:T(8,128)S(1)}) custom-call(s32[1]{0:T(128)S(6)} %copy.6.len_ref, bf16[8,128,128]{2,1,0:T(8,128)(2,1)S(1)} %spread.1.q_ref, bf16[8192,256]{1,0:T(8,128)(2,1)} %bitcast.14, bf16[16,256]{1,0:T(8,128)(2,1)} %bitcast.15), custom_call_target="tpu_custom_call" | custom-call | tf_op jit(solution)/shard_map/local/pallas_call | solution.py:149
  68.4 6.1 %all-to-all-done.1.got_ref = s16[32,32,128]{2,1,0:T(8,128)(2,1)S(1)} async-done(((s16[32,32,128]{2,1,0:T(8,128)(2,1)}), s16[32,32,128]{2,1,0:T(8,128)(2,1)S(1)}, u32[]{:S(2)}, u32[]{:S(2)}) %all-to-all-start.1) | async-done | bytes 262176 | tf_op jit(solution)/shard_map/all_to_all | solution.py:378
  74.5 1.7 %finish.1 = bf16[1,2,8192]{2,1,0:T(2,128)(2,1)} custom-call(s16[32,32,128]{2,1,0:T(8,128)(2,1)S(1)} %all-to-all-done.1.got_ref, f32[128,128]{1,0:T(8,128)S(1)} %get-tuple-element.21.numer_ref, f32[128,128]{1,0:T(8,128)S(1)} %get-tuple-element.22.stat_ref), custom_call_target="tpu_custom_call" | custom-call | tf_op jit(solution)/shard_map/finish/pallas_call | solution.py:331
Async XLA Ops:
  0.0 29.2 %collective-permute-start = (bf16[4096,256]{1,0:T(8,128)(2,1)}, bf16[4096,256]{1,0:T(8,128)(2,1)S(1)}, u32[]{:S(2)}, u32[]{:S(2)}) collective-permute-start(bf16[4096,256]{1,0:T(8,128)(2,1)} %bitcast.6), channel_id=1, source_target_pairs={{0,8},{8,0},{1,9},{9,1},{2,10},{10,2},{3,11},{11,3},{4,12},{12,4},... | collective-permute-start | bytes 6291464 | tf_op jit(solution)/shard_map/ppermute | solution.py:348
  26.4 9.0 %collective-permute-start.1 = (bf16[2,512,128]{2,1,0:T(8,128)(2,1)S(1)}, bf16[2,512,128]{2,1,0:T(8,128)(2,1)S(1)}, u32[]{:S(2)}, u32[]{:S(2)}) collective-permute-start(bf16[2,512,128]{2,1,0:T(8,128)(2,1)S(1)} %bitcast.10), channel_id=1, source_target_pairs={{0,192},{64,128},{128,64},{192,0},{1,193},{65,129},{129,65},{193,1... | collective-permute-start | bytes 786440 | tf_op jit(solution)/shard_map/ppermute | solution.py:358
  29.2 6.3 %copy-start = (bf16[4096,1,256]{2,0,1:T(8,128)(2,1)S(1)}, bf16[4096,1,256]{2,0,1:T(8,128)(2,1)}, u32[]{:S(2)}) copy-start(bf16[4096,1,256]{2,0,1:T(8,128)(2,1)} %param.6) | copy-start | bytes 6291460
  46.4 9.8 %collective-permute-start.3 = (s16[640,128]{1,0:T(8,128)(2,1)S(1)}, s16[640,128]{1,0:T(8,128)(2,1)S(1)}, u32[]{:S(2)}, u32[]{:S(2)}) collective-permute-start(s16[640,128]{1,0:T(8,128)(2,1)S(1)} %get-tuple-element.15), channel_id=1, source_target_pairs={{0,192},{64,128},{128,64},{192,0},{1,193},{65,129},{129,65},{193,1... | collective-permute-start | bytes 491528 | tf_op jit(solution)/shard_map/ppermute | solution.py:358
  49.0 7.6 %collective-permute-start.4 = (s16[640,128]{1,0:T(8,128)(2,1)S(1)}, s16[640,128]{1,0:T(8,128)(2,1)S(1)}, u32[]{:S(2)}, u32[]{:S(2)}) collective-permute-start(s16[640,128]{1,0:T(8,128)(2,1)S(1)} %get-tuple-element.16), channel_id=1, source_target_pairs={{0,128},{128,0},{1,129},{129,1},{2,130},{130,2},{3,131},{131,3},{4... | collective-permute-start | bytes 491528 | tf_op jit(solution)/shard_map/ppermute | solution.py:355
  49.0 8.0 %collective-permute-start.2 = (s16[640,128]{1,0:T(8,128)(2,1)S(1)}, s16[640,128]{1,0:T(8,128)(2,1)S(1)}, u32[]{:S(2)}, u32[]{:S(2)}) collective-permute-start(s16[640,128]{1,0:T(8,128)(2,1)S(1)} %document.3), channel_id=1, source_target_pairs={{0,64},{64,0},{1,65},{65,1},{2,66},{66,2},{3,67},{67,3},{4,68},{68... | collective-permute-start | bytes 491528 | tf_op jit(solution)/shard_map/ppermute | solution.py:372
  58.7 15.8 %all-to-all-start.1 = ((s16[32,32,128]{2,1,0:T(8,128)(2,1)}), s16[32,32,128]{2,1,0:T(8,128)(2,1)S(1)}, u32[]{:S(2)}, u32[]{:S(2)}) async-start(s16[32,32,128]{2,1,0:T(8,128)(2,1)} %merge.1), calls=%async_computation.1 | async-start | bytes 524288 | tf_op jit(solution)/shard_map/all_to_all | solution.py:378

commit v4 on v2

--- a/solution.py
+++ b/solution.py
@@ -14,6 +14,7 @@
 Y, ZL, CORE, X, ZH = 4, 4, 2, 4, 2
 AXES = ("y", "zl", "core", "x", "zh")
 WIDE = ("zl", "x", "zh")
+SWAP = [(0, 1), (1, 0)]
 BITS = 14.9
 FRACTION = 32767.0
 MASKED = -1e30
@@ -47,7 +48,7 @@
 
 def split_weight(weight):
     whole = toward_zero(weight * 0.5)
-    return whole, weight * (0.5 * FRACTION) - whole * FRACTION
+    return whole, (weight - 2.0 * whole) * (0.5 * FRACTION)
 
 
 def join_weight(whole, part):
@@ -285,16 +286,18 @@
             numer = term if numer is None else numer + term
         coded, power = code(numer)
         tile = side if b == 0 else shifted(side, -b)
-        tile = jnp.where(lane < 3 * blocks, tile, power).astype(jnp.int32).astype(jnp.int16)
+        tile = jnp.where(lane < 3 * blocks, tile, power)
         for s in range(owners):
             out_ref[b * owners + s, 0:16, :] = coded[16 * s : 16 * (s + 1), :]
-            out_ref[b * owners + s, 16:32, :] = tile[16 * s : 16 * (s + 1), :]
+            low, high = tile[16 * s : 16 * s + 8, :], shifted(tile[16 * s + 8 : 16 * s + 16, :], 16)
+            packed = jnp.where(lane[:8] < 16, low, high)
+            out_ref[b * owners + s, 16:24, :] = packed.astype(jnp.int32).astype(jnp.int16)
 
 
 def merge(parts):
     return pl.pallas_call(
         merge_kernel,
-        out_shape=jax.ShapeDtypeStruct((32, 32, LANES), jnp.int16),
+        out_shape=jax.ShapeDtypeStruct((32, 24, LANES), jnp.int16),
         in_specs=[VMEM] * len(parts),
         out_specs=VMEM,
         compiler_params=params(32),
@@ -304,13 +307,16 @@
 
 def finish_kernel(got_ref, numer_ref, stat_ref, out_ref, rows_ref, *, heads):
     steps = out_ref.shape[1]
-    rows = numer_ref.shape[0]
-
-    def read(z, first):
-        part = got_ref[z * heads : (z + 1) * heads, first : first + 16, :]
-        return part.astype(jnp.int32).astype(F32).reshape(rows, LANES)
-
-    tiles = [read(z, 16) for z in range(ZL)]
+    def read(z, first, count):
+        part = got_ref[z * heads : (z + 1) * heads, first : first + count, :]
+        return part.astype(jnp.int32).astype(F32).reshape(-1, LANES)
+
+    def unpack(packed):
+        moved = pltpu.roll(packed, LANES - 16, 1)
+        both = [part[8 * k : 8 * (k + 1)] for k in range(heads) for part in (packed, moved)]
+        return jnp.concatenate(both, axis=0)
+
+    tiles = [unpack(read(z, 16, 8)) for z in range(ZL)]
     peak = stat_ref[:, 0:1]
     tops = [t[:, 0:1] * 0.5 for t in tiles]
     top = functools.reduce(jnp.maximum, tops, peak)
@@ -320,7 +326,7 @@
     for z, t in enumerate(tiles):
         shrink = jnp.exp(tops[z] - top)
         weight = weight + shrink * join_weight(t[:, 4:5], t[:, 8:9])
-        numer = numer + read(z, 0) * (shrink * jnp.exp2(t[:, 12:13] - BITS))
+        numer = numer + read(z, 0, 16) * (shrink * jnp.exp2(t[:, 12:13] - BITS))
     rows_ref[...] = numer / weight
     for c in range(out_ref.shape[2] // LANES):
         out_ref[0, :, LANES * c : LANES * (c + 1)] = rows_ref[steps * c : steps * (c + 1), :].astype(BF16)
@@ -344,16 +350,21 @@
     heads = suffix_kv.shape[2]
     factor = math.log2(math.e) / math.sqrt(head_dim)
     kv_own = prefix_kv.reshape(positions, width)
-    kv_other = lax.ppermute(kv_own, "core", [(0, 1), (1, 0)])
+    kv_other = lax.ppermute(kv_own, "core", SWAP)
     spread_rows = spread(queries)
     gathered = lax.all_to_all(
-        spread_rows.reshape(ZL * heads, 16, LANES), WIDE, split_axis=0, concat_axis=0, tiled=True
+        spread_rows.reshape(ZL * heads, -1, LANES), WIDE, split_axis=0, concat_axis=0, tiled=True
     ).reshape(-1, LANES)
-    others = [lax.ppermute(gathered, "y", [(j, (j - d) % Y) for j in range(Y)]) for d in (1, 3, 2)]
+
+    def exchange(array, bits):
+        return lax.ppermute(array, "y", [(j, j ^ bits) for j in range(Y)])
+
+    others = [exchange(gathered, bits) for bits in (1, 3, 2)]
     parts = document(others[:1], kv_other, kv_own, factor, fetch=True)
     parts, others = lax.optimization_barrier((parts, others))
     parts += document(others[1:], kv_own, kv_other, factor)
-    parts = [lax.ppermute(p, "y", [(j, (j + d) % Y) for j in range(Y)]) for d, p in zip((1, 3, 2), parts)]
+    parts = lax.optimization_barrier(parts)
+    parts = [exchange(part, bits) for bits, part in zip((1, 3, 2), parts)]
     parts += document([gathered], kv_own, kv_other, factor)
     merged = merge(parts)
     merged, spread_rows = lax.optimization_barrier((merged, spread_rows))
@@ -366,7 +377,7 @@
 def solution(mesh):
     devices = mesh.devices.reshape(Y, ZL, CORE, X, ZH)
     fine = Mesh(devices, AXES)
-    prefix, sample = ("y", "zl", "core"), ("x", "zh")
+    prefix, sample = AXES[:3], AXES[3:]
     owner = P(prefix + sample)
     in_specs = (owner, P(prefix, sample), owner, owner, owner)
     return jax.shard_map(per_device, mesh=fine, in_specs=in_specs, out_specs=owner, check_vma=False)

time: 76.5 us -> 74.5 us (0.974)
  starting transfers between devices: 16.5 us -> 14.4 us
    ppermute x7, starting transfers between devices: 12.3 us -> 9.94 us  [the longest x6 9.94 us: exchange(): return lax.ppermute(array, 'y', [(j, j ^ bits) for j in range(Y)])]
  transfers between devices with their start and end apart: 8 -> 8, of which waited for: 2 -> 2; matrix products, arithmetic and copies ran while one was open for 0% -> 0% of each run, Pallas kernels for 36% -> 23%
where the time goes in v4:
time: 74.5 us; the launch traced here: 74.2 us
  Pallas kernels  31.6 us (42%)
  blocking collectives  21.5 us (29%)
  starting transfers between devices  14.4 us (19%)
  waiting for transfers between devices  5.94 us (8%)
    pallas_call x3, Pallas kernels, document(): pl.pallas_call(functools.partial(document_kernel, groups=len(groups), fet...  22.6 us
    all_to_all x1, blocking collectives, per_device(): lax.all_to_all(spread_rows.reshape(ZL * heads, -1, LANES), WIDE, split_ax...  21.5 us
    ppermute x6, starting transfers between devices, exchange(): return lax.ppermute(array, 'y', [(j, j ^ bits) for j in range(Y)])  9.94 us
    all_to_all x1, waiting for transfers between devices, per_device(): got = lax.all_to_all(merged, WIDE, split_axis=0, concat_axis=0, tiled=True)  5.43 us
    all_to_all x1, starting transfers between devices, per_device(): got = lax.all_to_all(merged, WIDE, split_axis=0, concat_axis=0, tiled=True)  4.49 us
    pallas_call x1, Pallas kernels, local(): pl.pallas_call(functools.partial(local_kernel, heads=heads, chunk=512, fa...  4.44 us
    pallas_call x1, Pallas kernels, merge(): pl.pallas_call(merge_kernel, out_shape=jax.ShapeDtypeStruct((32, 24, LANE...  1.99 us
    pallas_call x1, Pallas kernels, finish(): pl.pallas_call(functools.partial(finish_kernel, heads=heads), out_shape=j...  1.74 us
  transfers between devices with their start and end apart: 8, of which 2 were waited for; matrix products, arithmetic and copies ran while one was open for 0% of the time, Pallas kernels for 23%

profile of v4, /device:TPU:32, one launch (start us, length us, event | category | flops | bytes accessed | tf_op | source)
XLA Modules:
  0.0 74.2 jit_solution(11941072629082749184)
XLA Ops:
  0.0 0.0 collective-permute-start.1
  0.0 0.8 %spread.1.q_ref = bf16[4,128,128]{2,1,0:T(8,128)(2,1)S(1)} custom-call(bf16[1,2,8192]{2,1,0:T(2,128)(2,1)} %q_ref.1), custom_call_target="tpu_custom_call" | custom-call | tf_op jit(solution)/shard_map/spread/pallas_call | solution.py:73
  0.8 21.5 %all_to_all.10 = bf16[32,16,128]{2,1,0:T(8,128)(2,1)S(1)} all-to-all(bf16[32,16,128]{2,1,0:T(8,128)(2,1)S(1)} %bitcast.9), channel_id=1, replica_groups=mesh['y'=4,'zl'=4,'core'=2,'x'=4,'zh'=2] {'zl','x','zh'}, dimensions={0} | all-to-all | bytes 262144 | tf_op jit(solution)/shard_map/all_to_all | solution.py:355
  22.3 0.0 copy-start
  22.3 1.6 %collective-permute-start = (bf16[512,128]{1,0:T(8,128)(2,1)S(1)}, bf16[512,128]{1,0:T(8,128)(2,1)S(1)}, u32[]{:S(2)}, u32[]{:S(2)}) collective-permute-start(bf16[512,128]{1,0:T(8,128)(2,1)S(1)} %bitcast.10), channel_id=1, source_target_pairs={{0,64},{64,0},{128,192},{192,128},{1,65},{65,1},{129,193},{193,129... | collective-permute-start | bytes 393224 | tf_op jit(solution)/shard_map/ppermute | solution.py:360
  23.9 2.2 %collective-permute-start.2 = (bf16[512,128]{1,0:T(8,128)(2,1)S(1)}, bf16[512,128]{1,0:T(8,128)(2,1)S(1)}, u32[]{:S(2)}, u32[]{:S(2)}) collective-permute-start(bf16[512,128]{1,0:T(8,128)(2,1)S(1)} %bitcast.11), channel_id=1, source_target_pairs={{0,192},{64,128},{128,64},{192,0},{1,193},{65,129},{129,65},{193,1... | collective-permute-start | bytes 393224 | tf_op jit(solution)/shard_map/ppermute | solution.py:360
  26.1 0.7 collective-permute-start.3
  26.8 0.5 collective-permute-done.refs_0_
  27.3 0.0 collective-permute-done.1.refs_1_.refs_3_.refs_2_
  27.3 6.2 %document.3 = s16[640,128]{1,0:T(8,128)(2,1)S(1)} custom-call(bf16[512,128]{1,0:T(8,128)(2,1)S(1)} %collective-permute-done.refs_0_, bf16[4096,256]{1,0:T(8,128)(2,1)S(1)} %collective-permute-done.1.refs_1_.refs_3_.refs_2_, bf16[4096,256]{1,0:T(8,128)(2,1)} %bitcast.6), custom_call_target="tpu_custom_call" | custom-call | tf_op jit(solution)/shard_map/document/pallas_call | solution.py:252
  33.6 0.0 collective-permute-done.2.refs_0_
  33.6 0.0 collective-permute-done.3.refs_1_
  33.6 0.0 copy-done
  33.6 10.8 %document.4 = (s16[640,128]{1,0:T(8,128)(2,1)S(1)}, s16[640,128]{1,0:T(8,128)(2,1)S(1)}) custom-call(bf16[512,128]{1,0:T(8,128)(2,1)S(1)} %collective-permute-done.2.refs_0_, bf16[512,128]{1,0:T(8,128)(2,1)S(1)} %collective-permute-done.3.refs_1_, bf16[4096,256]{1,0:T(8,128)(2,1)S(1)} %bitcast.7, ...), custom_call_target="tpu_custom_call" | custom-call | tf_op jit(solution)/shard_map/document/pallas_call | solution.py:252
  44.4 2.1 %collective-permute-start.4 = (s16[640,128]{1,0:T(8,128)(2,1)S(1)}, s16[640,128]{1,0:T(8,128)(2,1)S(1)}, u32[]{:S(2)}, u32[]{:S(2)}) collective-permute-start(s16[640,128]{1,0:T(8,128)(2,1)S(1)} %document.3), channel_id=1, source_target_pairs={{0,64},{64,0},{128,192},{192,128},{1,65},{65,1},{129,193},{193,129... | collective-permute-start | bytes 491528 | tf_op jit(solution)/shard_map/ppermute | solution.py:360
  46.5 2.0 %collective-permute-start.5 = (s16[640,128]{1,0:T(8,128)(2,1)S(1)}, s16[640,128]{1,0:T(8,128)(2,1)S(1)}, u32[]{:S(2)}, u32[]{:S(2)}) collective-permute-start(s16[640,128]{1,0:T(8,128)(2,1)S(1)} %get-tuple-element.23), channel_id=1, source_target_pairs={{0,192},{64,128},{128,64},{192,0},{1,193},{65,129},{129,65},{193,1... | collective-permute-start | bytes 491528 | tf_op jit(solution)/shard_map/ppermute | solution.py:360
  48.5 1.3 %collective-permute-start.6 = (s16[640,128]{1,0:T(8,128)(2,1)S(1)}, s16[640,128]{1,0:T(8,128)(2,1)S(1)}, u32[]{:S(2)}, u32[]{:S(2)}) collective-permute-start(s16[640,128]{1,0:T(8,128)(2,1)S(1)} %get-tuple-element.24), channel_id=1, source_target_pairs={{0,128},{64,192},{128,0},{192,64},{1,129},{65,193},{129,1},{193,65... | collective-permute-start | bytes 491528 | tf_op jit(solution)/shard_map/ppermute | solution.py:360
  49.9 5.5 %document.5.refs_3_ = s16[640,128]{1,0:T(8,128)(2,1)S(1)} custom-call(bf16[512,128]{1,0:T(8,128)(2,1)S(1)} %bitcast.13, bf16[4096,256]{1,0:T(8,128)(2,1)S(1)} %bitcast.8, bf16[4096,256]{1,0:T(8,128)(2,1)S(1)} %collective-permute-done.1.refs_1_.refs_3_.refs_2_), custom_call_target="tpu_custom_call" | custom-call | tf_op jit(solution)/shard_map/document/pallas_call | solution.py:252
  55.4 0.0 collective-permute-done.4.refs_0_
  55.4 0.0 collective-permute-done.5.refs_1_
  55.4 0.0 collective-permute-done.6.refs_2_
  55.4 2.0 %merge.1 = s16[32,24,128]{2,1,0:T(8,128)(2,1)} custom-call(s16[640,128]{1,0:T(8,128)(2,1)S(1)} %collective-permute-done.4.refs_0_, s16[640,128]{1,0:T(8,128)(2,1)S(1)} %collective-permute-done.5.refs_1_, s16[640,128]{1,0:T(8,128)(2,1)S(1)} %collective-permute-done.6.refs_2_, s16[640,128]{1,0:T(8,128)(2,1)S(1)} %document.5.refs_3_), custom_call_target="tpu_custom_call" | custom-call | tf_op jit(solution)/shard_map/merge/pallas_call | solution.py:298
  57.4 4.5 %all-to-all-start.1 = ((s16[32,24,128]{2,1,0:T(8,128)(2,1)}), s16[32,24,128]{2,1,0:T(8,128)(2,1)S(1)}, u32[]{:S(2)}, u32[]{:S(2)}) async-start(s16[32,24,128]{2,1,0:T(8,128)(2,1)} %merge.1), calls=%async_computation.1 | async-start | bytes 393216 | tf_op jit(solution)/shard_map/all_to_all | solution.py:371
  62.6 4.4 %local.1 = (f32[128,128]{1,0:T(8,128)S(1)}, f32[128,128]{1,0:T(8,128)S(1)}) custom-call(s32[1]{0:T(128)S(6)} %copy.6.len_ref, bf16[4,128,128]{2,1,0:T(8,128)(2,1)S(1)} %spread.1.q_ref, bf16[8192,256]{1,0:T(8,128)(2,1)} %bitcast.14, bf16[16,256]{1,0:T(8,128)(2,1)} %bitcast.15), custom_call_target="tpu_custom_call" | custom-call | tf_op jit(solution)/shard_map/local/pallas_call | solution.py:149
  67.0 5.4 %all-to-all-done.1.got_ref = s16[32,24,128]{2,1,0:T(8,128)(2,1)S(1)} async-done(((s16[32,24,128]{2,1,0:T(8,128)(2,1)}), s16[32,24,128]{2,1,0:T(8,128)(2,1)S(1)}, u32[]{:S(2)}, u32[]{:S(2)}) %all-to-all-start.1) | async-done | bytes 196640 | tf_op jit(solution)/shard_map/all_to_all | solution.py:371
  72.5 1.7 %finish.1 = bf16[1,2,8192]{2,1,0:T(2,128)(2,1)} custom-call(s16[32,24,128]{2,1,0:T(8,128)(2,1)S(1)} %all-to-all-done.1.got_ref, f32[128,128]{1,0:T(8,128)S(1)} %get-tuple-element.27.numer_ref, f32[128,128]{1,0:T(8,128)S(1)} %get-tuple-element.28.stat_ref), custom_call_target="tpu_custom_call" | custom-call | tf_op jit(solution)/shard_map/finish/pallas_call | solution.py:336
Async XLA Ops:
  0.0 27.3 %collective-permute-start.1 = (bf16[4096,256]{1,0:T(8,128)(2,1)}, bf16[4096,256]{1,0:T(8,128)(2,1)S(1)}, u32[]{:S(2)}, u32[]{:S(2)}) collective-permute-start(bf16[4096,256]{1,0:T(8,128)(2,1)} %bitcast.5), channel_id=1, source_target_pairs={{0,8},{8,0},{1,9},{9,1},{2,10},{10,2},{3,11},{11,3},{4,12},{12,4},... | collective-permute-start | bytes 6291464 | tf_op jit(solution)/shard_map/ppermute | solution.py:353
  22.3 11.2 %copy-start = (bf16[4096,1,256]{2,0,1:T(8,128)(2,1)S(1)}, bf16[4096,1,256]{2,0,1:T(8,128)(2,1)}, u32[]{:S(2)}) copy-start(bf16[4096,1,256]{2,0,1:T(8,128)(2,1)} %param.6) | copy-start | bytes 6291460
  22.3 5.0 %collective-permute-start = (bf16[512,128]{1,0:T(8,128)(2,1)S(1)}, bf16[512,128]{1,0:T(8,128)(2,1)S(1)}, u32[]{:S(2)}, u32[]{:S(2)}) collective-permute-start(bf16[512,128]{1,0:T(8,128)(2,1)S(1)} %bitcast.10), channel_id=1, source_target_pairs={{0,64},{64,0},{128,192},{192,128},{1,65},{65,1},{129,193},{193,129... | collective-permute-start | bytes 393224 | tf_op jit(solution)/shard_map/ppermute | solution.py:360
  23.9 9.6 %collective-permute-start.2 = (bf16[512,128]{1,0:T(8,128)(2,1)S(1)}, bf16[512,128]{1,0:T(8,128)(2,1)S(1)}, u32[]{:S(2)}, u32[]{:S(2)}) collective-permute-start(bf16[512,128]{1,0:T(8,128)(2,1)S(1)} %bitcast.11), channel_id=1, source_target_pairs={{0,192},{64,128},{128,64},{192,0},{1,193},{65,129},{129,65},{193,1... | collective-permute-start | bytes 393224 | tf_op jit(solution)/shard_map/ppermute | solution.py:360
  26.1 7.5 %collective-permute-start.3 = (bf16[512,128]{1,0:T(8,128)(2,1)S(1)}, bf16[512,128]{1,0:T(8,128)(2,1)S(1)}, u32[]{:S(2)}, u32[]{:S(2)}) collective-permute-start(bf16[512,128]{1,0:T(8,128)(2,1)S(1)} %bitcast.12), channel_id=1, source_target_pairs={{0,128},{64,192},{128,0},{192,64},{1,129},{65,193},{129,1},{193,65... | collective-permute-start | bytes 393224 | tf_op jit(solution)/shard_map/ppermute | solution.py:360
  44.4 11.0 %collective-permute-start.4 = (s16[640,128]{1,0:T(8,128)(2,1)S(1)}, s16[640,128]{1,0:T(8,128)(2,1)S(1)}, u32[]{:S(2)}, u32[]{:S(2)}) collective-permute-start(s16[640,128]{1,0:T(8,128)(2,1)S(1)} %document.3), channel_id=1, source_target_pairs={{0,64},{64,0},{128,192},{192,128},{1,65},{65,1},{129,193},{193,129... | collective-permute-start | bytes 491528 | tf_op jit(solution)/shard_map/ppermute | solution.py:360
  46.5 8.9 %collective-permute-start.5 = (s16[640,128]{1,0:T(8,128)(2,1)S(1)}, s16[640,128]{1,0:T(8,128)(2,1)S(1)}, u32[]{:S(2)}, u32[]{:S(2)}) collective-permute-start(s16[640,128]{1,0:T(8,128)(2,1)S(1)} %get-tuple-element.23), channel_id=1, source_target_pairs={{0,192},{64,128},{128,64},{192,0},{1,193},{65,129},{129,65},{193,1... | collective-permute-start | bytes 491528 | tf_op jit(solution)/shard_map/ppermute | solution.py:360
  48.5 6.9 %collective-permute-start.6 = (s16[640,128]{1,0:T(8,128)(2,1)S(1)}, s16[640,128]{1,0:T(8,128)(2,1)S(1)}, u32[]{:S(2)}, u32[]{:S(2)}) collective-permute-start(s16[640,128]{1,0:T(8,128)(2,1)S(1)} %get-tuple-element.24), channel_id=1, source_target_pairs={{0,128},{64,192},{128,0},{192,64},{1,129},{65,193},{129,1},{193,65... | collective-permute-start | bytes 491528 | tf_op jit(solution)/shard_map/ppermute | solution.py:360
  57.4 15.0 %all-to-all-start.1 = ((s16[32,24,128]{2,1,0:T(8,128)(2,1)}), s16[32,24,128]{2,1,0:T(8,128)(2,1)S(1)}, u32[]{:S(2)}, u32[]{:S(2)}) async-start(s16[32,24,128]{2,1,0:T(8,128)(2,1)} %merge.1), calls=%async_computation.1 | async-start | bytes 393216 | tf_op jit(solution)/shard_map/all_to_all | solution.py:371
